TPU v7x, 32 devices: a whole 2x2x4 slice. The times are simulated.
32 devices in a mesh: strip: 8 (over y, x, core), lag: 4 (over z).
Axes of the slice: x: 2, y: 2, z: 4, core: 2. Of those that a mesh axis runs over, the one named last changes fastest.
Arguments:
- image_grad: float32 [128, 512, 1024], P('lag', 'strip'), may hold values from -0.4 to 0.4
- source_field: float32 [2, 512, 1024], P(None, None, 'strip'), may hold values from -6 to 6
- receiver_field: float32 [2, 512, 1024], P(None, None, 'strip'), may hold values from -6 to 6
Outputs:
- source_adjoint: float32 [2, 512, 1024], P(None, 'strip', 'lag')
- receiver_adjoint: float32 [2, 512, 1024], P(None, 'strip', 'lag')
All inputs are finite; a program needn't handle non-finite values.
Results may differ from a plain program's by a relative error of at most 0.0003.
Values sent between devices are 32-bit elements; how exact they have to be, the bound alone decides.
No kernel may reach another device: no remote copies, remote signals or barrier semaphores. Data moves between devices by JAX's collectives and lax.ppermute only.
A program may use at most 128 MiB of HBM per device.

v0:
```python
import functools

import jax
import jax.numpy as jnp
from jax import lax
from jax.experimental import pallas as pl
from jax.experimental.pallas import tpu as pltpu
from jax.sharding import PartitionSpec as P

LANES = 128
ROWS = 8
CLASSES = 4
PAIRS = 4
CHUNK = 512
ALONE = 1
FIRST_FORM = "direct"
SECOND_FORM = "halves"
ORDERED = True
GRAD_IN_HBM = True
FILTER_COST = 3 * 10**9
FIRST_COST = 0
SECOND_COST = 10**9
FILTER_BYTES = 32 * 1024 * 1024
SUM_BYTES = 8 * 1024 * 1024
SMALL_BYTES = 4 * 1024 * 1024

def weight(size):
    return pl.CostEstimate(flops=size, bytes_accessed=size, transcendentals=0)


def in_hbm(array):
    return pltpu.with_memory_space_constraint(array, pltpu.HBM)


whole_vmem = pl.BlockSpec(memory_space=pltpu.VMEM)


def filter_kernel(pad, grad_hbm, near_ref, next_ref, out_ref, edge_parts, held, sems, *turned):
    lag_count, depth, width = grad_hbm.shape
    half = lag_count // 2
    tiles = width // LANES
    steps = half // PAIRS

    def fetch(step, side):
        lags = pl.ds(step * PAIRS + side * half, PAIRS)
        return pltpu.make_async_copy(grad_hbm.at[lags], held.at[lags], sems.at[2 * step + side])

    for step in range(steps):
        for side in range(2):
            fetch(step, side).start()

    centers = turned
    strip = lax.axis_index("strip")
    core = lax.rem(strip, 2)
    inside = (strip != 0) & (strip != lax.axis_size("strip") - 1)
    blank = jnp.zeros((LANES - 2 * lag_count, LANES), jnp.float32)

    def split(value):
        high = value.astype(jnp.bfloat16)
        return high, (value - high.astype(jnp.float32)).astype(jnp.bfloat16)

    for t in range(tiles):
        rows = pl.ds(t * lag_count, lag_count)
        near, following = near_ref[rows], jnp.where(inside, next_ref[rows], 0.0)
        above = jnp.where(core == 0, following, near)
        below = jnp.where(core == 0, near, following)
        parts = split(jnp.concatenate([above, below, blank], 0).T)
        for part in range(2):
            edge_parts[part, pl.ds(t * LANES, LANES)] = parts[part]
    out_ref[:, pl.ds(0, pad)] = jnp.zeros((half, pad, LANES), jnp.float32)
    out_ref[:, pl.ds(pad + width, pad)] = jnp.zeros((half, pad, LANES), jnp.float32)
    for center_t in centers:
        center_t[pl.ds(0, ROWS)] = jnp.zeros((ROWS, LANES), jnp.float32)
        center_t[pl.ds(ROWS + width, ROWS)] = jnp.zeros((ROWS, LANES), jnp.float32)

    def body(step, carry):
        fetch(step, 0).wait()
        fetch(step, 1).wait()
        low_ref, high_ref = held.at[pl.ds(step * PAIRS, PAIRS)], held.at[pl.ds(step * PAIRS + half, PAIRS)]
        source = lax.broadcasted_iota(jnp.int32, (LANES, LANES), 0)
        target = lax.broadcasted_iota(jnp.int32, (LANES, LANES), 1)
        beside = (jnp.abs(source - target) == 1) & ((source < depth) == (target < depth))
        band = jnp.where(source == target, 2.0, jnp.where(beside, -0.25, 0.0))
        upper = jnp.where(target == 0, 0, jnp.where(target == depth, half, 2 * LANES))
        lower = jnp.where(target == depth - 1, 0, jnp.where(target == 2 * depth - 1, half, 2 * LANES))
        matrices = []
        for within in range(PAIRS):
            lag = step * PAIRS + within
            chosen = (source == upper + lag) | (source == lower + lag + lag_count)
            choice = jnp.where(chosen, -0.25, 0.0)
            matrices.append(jnp.concatenate([band, choice], 0).astype(jnp.bfloat16))

        def turn(within, t):
            rows = pl.ds(t * LANES, LANES)
            center = jnp.concatenate([low_ref[within, :, rows], high_ref[within, :, rows]], 0).T
            centers[within][pl.ds(ROWS + t * LANES, LANES)] = center

        def join(within, at):
            rows = pl.ds(at * chunk, chunk)
            west = centers[within][pl.ds(ROWS - 1 + at * chunk, chunk)]
            east = centers[within][pl.ds(ROWS + 1 + at * chunk, chunk)]
            parts = split(centers[within][pl.ds(ROWS + at * chunk, chunk)])
            products = [
                jnp.dot(
                    jnp.concatenate([parts[part], edge_parts[part, rows]], 1),
                    matrices[within],
                    preferred_element_type=jnp.float32,
                )
                for part in range(2)
            ]
            value = (products[0] + products[1]) - 0.25 * (west + east)
            out_ref[step * PAIRS + within, pl.ds(pad + at * chunk, chunk)] = value

        chunk = min(CHUNK, width)
        for within in range(PAIRS + 1):
            for t in range(tiles):
                if within < PAIRS:
                    turn(within, t)
                if within and (t + 1) * LANES % chunk == 0:
                    join(within - 1, ((t + 1) * LANES // chunk) - 1)
        return carry

    lax.fori_loop(0, steps, body, 0)


def filter_slabs(image_grad, from_near, from_next, pad):
    lag_count, depth, width = image_grad.shape
    return pl.pallas_call(
        functools.partial(filter_kernel, pad),
        out_shape=jax.ShapeDtypeStruct((lag_count // 2, width + 2 * pad, 2 * depth), jnp.float32),
        in_specs=[pl.BlockSpec(memory_space=pltpu.HBM if GRAD_IN_HBM else pl.ANY), whole_vmem, whole_vmem],
        out_specs=whole_vmem,
        scratch_shapes=[pltpu.VMEM((2, width, LANES), jnp.bfloat16)]
        + [pltpu.VMEM(image_grad.shape, jnp.float32), pltpu.SemaphoreType.DMA((lag_count // PAIRS,))]
        + [pltpu.VMEM((width + 2 * ROWS, LANES), jnp.float32)] * PAIRS,
        compiler_params=pltpu.CompilerParams(vmem_limit_bytes=FILTER_BYTES),
        cost_estimate=weight(FILTER_COST),
        name="filter_slabs",
    )(in_hbm(image_grad) if GRAD_IN_HBM else image_grad, from_near, from_next)


def sum_kernel(sign, places, where_at, blocks, slab_ref, *refs):
    number = len(blocks)
    pieces, outs = refs[: -3 - number], refs[-3 - number : -3]
    field_ref, paired, acc = refs[-3:]
    half, slab_rows, _ = slab_ref.shape
    width = field_ref.shape[0]
    if where_at is None:
        field_ref[...] = pieces[0][...]
    else:
        strip = lax.axis_index("strip")
        for index, row, distance in where_at:
            rows = pl.multiple_of((strip ^ distance) * LANES, LANES)
            field_ref[pl.ds(rows, LANES)] = pieces[index][pl.ds(row, LANES)]
    pad = (slab_rows - width) // 2
    lag_count = 2 * half
    margin = 2 * pad + 2 * half
    place = lax.axis_index("lag")
    first = place * lag_count - pad
    spread = width + half
    block_rows = ROWS * max(m for m in range(1, 11) if spread // ROWS % m == 0)
    low_at = 0 if sign > 0 else half
    high_at = half - low_at

    for snap in range(2):
        blank = jnp.zeros((margin + half, LANES), jnp.float32)
        paired[snap, pl.ds(0, margin)] = blank[:margin]
        paired[snap, pl.ds(margin + width, margin)] = blank[:margin]
    low = lax.broadcasted_iota(jnp.int32, (LANES, LANES), 1) < LANES // 2
    edge = jnp.zeros((half, LANES), jnp.float32)
    field = field_ref[...]
    lower = lax.broadcasted_iota(jnp.int32, (spread, LANES), 1) < LANES // 2
    if sign > 0:
        here = jnp.concatenate([edge, field], 0)
        there = jnp.concatenate([field, edge], 0)
        start = margin - half
    else:
        here = jnp.concatenate([field, edge], 0)
        there = jnp.concatenate([edge, field], 0)
        start = margin
    paired[0, pl.ds(start, spread)] = jnp.where(lower, here, pltpu.roll(there, LANES // 2, 1))
    paired[1, pl.ds(start, spread)] = jnp.where(lower, pltpu.roll(here, LANES // 2, 1), there)

    tall = block_rows // ROWS
    per_class = half // CLASSES

    def block(at, carry):
        y = at * block_rows - low_at
        slab_at = pl.multiple_of(pad + y + sign * first, ROWS)
        field_at = pl.multiple_of(margin + y + sign * 2 * first, ROWS)
        totals = [[None] * tall for _ in range(2)]
        for cls in range(CLASSES):
            held = {}
            for step in range(per_class):
                lag = step * CLASSES + cls
                for up in range(tall):
                    slab = slab_ref[lag, pl.ds(slab_at + sign * lag + up * ROWS, ROWS)]
                    for snap in range(2):
                        row = sign * 2 * lag + up * ROWS
                        if (snap, row) not in held:
                            held[snap, row] = paired[snap, pl.ds(field_at + row, ROWS)]
                        term = slab * held[snap, row]
                        total = totals[snap][up]
                        totals[snap][up] = term if total is None else total + term
        for snap in range(2):
            for up in range(tall):
                rows = pl.multiple_of(at * block_rows + up * ROWS, ROWS)
                acc[snap, pl.ds(rows, ROWS)] = totals[snap][up]
        return carry

    lax.fori_loop(0, spread // block_rows, block, 0)

    part = width // places

    def finish(target, slot, source):
        for piece in range(part // LANES):
            x = pl.multiple_of(source * part + piece * LANES, LANES)
            at_low = pl.ds(x + low_at, LANES)
            at_high = pl.ds(x + high_at, LANES)
            straight = jnp.where(low, acc[0, at_low], acc[1, at_high])
            crossed = jnp.where(low, acc[1, at_low], acc[0, at_high])
            rows = pl.ds(slot * part + piece * LANES, LANES)
            target[rows] = straight + pltpu.roll(crossed, LANES // 2, 1)

    for target, distances in zip(outs, blocks):
        for slot, distance in enumerate(distances):
            finish(target, slot, place ^ distance)


BLOCKS = {
    "direct": ((0,), (1,), (2,), (3,)),
    "halves": ((0, 3), (1, 2)),
    "forward": ((0,), (2,), (3, 1), (3,)),
}


def sum_lags(sign, form, slabs, pieces, where_at, width, after=()):
    half, slab_rows, _ = slabs.shape
    pad = (slab_rows - width) // 2
    margin = 2 * pad + 2 * half
    places = lax.axis_size("lag")
    part = width // places
    out_shape = [jax.ShapeDtypeStruct((len(held) * part, LANES), jnp.float32) for held in BLOCKS[form]]
    return pl.pallas_call(
        functools.partial(sum_kernel, sign, places, where_at, BLOCKS[form]),
        out_shape=out_shape,
        in_specs=[whole_vmem] * (1 + len(pieces) + len(after)),
        out_specs=[whole_vmem] * len(out_shape),
        scratch_shapes=[
            pltpu.VMEM((width, LANES), jnp.float32),
            pltpu.VMEM((2, width + 2 * margin, LANES), jnp.float32),
            pltpu.VMEM((2, width + half, LANES), jnp.float32),
        ],
        compiler_params=pltpu.CompilerParams(vmem_limit_bytes=SUM_BYTES),
        cost_estimate=weight(FIRST_COST if sign > 0 else SECOND_COST),
        name="sum_lags",
    )(slabs, *pieces, *after)


def send_kernel(pieces, grad_hbm, *refs):
    lag_count, depth, width = grad_hbm.shape
    tiles = width // LANES
    number = (len(refs) - 4) // 3
    fields, near_ref, next_ref = refs[:number], refs[number], refs[number + 1]
    mine = refs[number + 2 : 2 * number + 2]
    held, edges, sems = refs[2 * number + 2 : 3 * number + 2], refs[-2], refs[-1]
    strip = lax.axis_index("strip")
    core = lax.rem(strip, 2)
    copies = []
    for side in range(2):
        rows = pl.ds(side * (depth - ROWS), ROWS)
        copies.append(pltpu.make_async_copy(grad_hbm.at[:, rows], edges.at[side], sems.at[side]))
    for f in range(number):
        copies.append(pltpu.make_async_copy(fields[f], held[f], sems.at[2 + f]))
    for copy in copies:
        copy.start()

    for f in range(number):
        copies[2 + f].wait()
        snaps = held[f].shape[0]
        for at in range(pieces):
            for side in range(2):
                first = pl.multiple_of((strip ^ (2 * at + side)) * depth, depth)
                rows = [held[f][s, pl.ds(first, depth)] for s in range(snaps)]
                piece = jnp.concatenate(rows, 0).T
                if side:
                    start = lag_count * tiles + (f * pieces + at) * LANES
                    near_ref[pl.ds(start, LANES)] = piece
                else:
                    mine[f][pl.ds(at * LANES, LANES)] = piece

    copies[0].wait()
    copies[1].wait()
    low = core == 0
    for t in range(tiles):
        lanes = pl.ds(t * LANES, LANES)
        top = edges[0, :, 0, lanes]
        bottom = edges[1, :, ROWS - 1, lanes]
        rows = pl.ds(t * lag_count, lag_count)
        near_ref[rows] = jnp.where(low, bottom, top)
        next_ref[rows] = jnp.where(low, top, bottom)


def pack_kernel(pieces, edge_rows, sends, *refs):
    number = 1 + max(f for _, group in sends for f in group)
    mine, near_ref, out = refs[:number], refs[number], refs[number + 1 :]
    for (at, group), out_ref in zip(sends, out):
        for place, f in enumerate(group):
            rows = pl.ds(at * LANES, LANES)
            out_ref[pl.ds(2 * place * LANES, LANES)] = mine[f][rows]
            far = pl.ds(edge_rows + (f * pieces + at) * LANES, LANES)
            out_ref[pl.ds((2 * place + 1) * LANES, LANES)] = near_ref[far]


def strip_swap(part, distance):
    count = lax.axis_size("strip")
    return lax.ppermute(part, "strip", [(i, i ^ distance) for i in range(count)])


def gather_rows(image_grad, fields):
    lag_count, depth, width = image_grad.shape
    count = lax.axis_size("strip")
    snaps, all_rows, columns = fields[0].shape
    direct = columns == LANES and count >= 4 and count & (count - 1) == 0
    pieces = count // 2 if direct else 0
    number = len(fields) if direct else 0
    edge_rows = lag_count * (width // LANES)

    def buffer(rows):
        return jax.ShapeDtypeStruct((rows, LANES), jnp.float32)

    near, following, *mine = pl.pallas_call(
        functools.partial(send_kernel, pieces),
        out_shape=[buffer(edge_rows + number * pieces * LANES), buffer(edge_rows)]
        + [buffer(pieces * LANES)] * number,
        in_specs=[pl.BlockSpec(memory_space=pltpu.HBM)] * (1 + number),
        out_specs=[whole_vmem] * (2 + number),
        scratch_shapes=[pltpu.VMEM(f.shape, jnp.float32) for f in fields[:number]]
        + [pltpu.VMEM((2, lag_count, ROWS, width), jnp.float32), pltpu.SemaphoreType.DMA((2 + number,))],
        compiler_params=pltpu.CompilerParams(vmem_limit_bytes=SUM_BYTES),
        name="send_rows",
    )(*(in_hbm(a) for a in (image_grad, *fields[:number])))
    near = strip_swap(near, 1)
    following = lax.ppermute(
        following, "strip", [p for i in range(1, count, 2) for p in ((i, (i + 1) % count), ((i + 1) % count, i))]
    )
    if not direct:
        whole = []
        for field in fields:
            cut = field.reshape(snaps, count, depth, columns).transpose(1, 3, 0, 2)
            cut = lax.all_to_all(cut.reshape(count, columns, snaps * depth), "strip", 0, 0, tiled=True)
            whole.append([cut.reshape(count * columns, snaps * depth)])
        return near, following, whole, [None] * len(fields)

    everything = tuple(range(number))
    sends = [(at, everything) for at in range(1, pieces - ALONE)]
    sends += [(at, (f,)) for f in everything for at in range(pieces - ALONE, pieces)]
    out_shape = [buffer(2 * len(group) * LANES) for _, group in sends]
    packed = pl.pallas_call(
        functools.partial(pack_kernel, pieces, edge_rows, sends),
        out_shape=out_shape,
        in_specs=[whole_vmem] * (number + 1),
        out_specs=[whole_vmem] * len(out_shape),
        compiler_params=pltpu.CompilerParams(vmem_limit_bytes=SMALL_BYTES),
        name="pack_fields",
    )(*mine, near)
    sent = [strip_swap(part, 2 * at) for (at, _), part in zip(sends, packed)]
    whole, where_at = [], []
    for f in range(number):
        came = [(at, group.index(f), part) for (at, group), part in zip(sends, sent) if f in group]
        whole.append([mine[f], near] + [part for _, _, part in came])
        where_at.append([(0, 0, 0), (1, edge_rows + f * pieces * LANES, 1)])
        for index, (at, place, _) in enumerate(came):
            for side in range(2):
                where_at[f].append((2 + index, (2 * place + side) * LANES, 2 * at + side))
    return near, following, whole, where_at


def exchange(parts, distance):
    count = lax.axis_size("lag")
    return lax.ppermute(parts, "lag", [(i, i ^ distance) for i in range(count)])


def turn_back_kernel(*refs):
    out_ref = refs[-1]
    snaps, depth, width = out_ref.shape
    for at in range(width // LANES):
        rows = pl.ds(at * LANES, LANES)
        total = refs[0][rows]
        for ref in refs[1:-1]:
            total = total + ref[rows]
        turned = total.T
        for snap in range(snaps):
            out_ref[snap, :, rows] = turned[snap * depth : (snap + 1) * depth]


def lag_send(part, *pairs):
    return lax.ppermute(part, "lag", pairs)


def sum_places(form, parts, snaps):
    if form == "direct":
        terms = [parts[0]] + [exchange(part, d) for d, part in enumerate(parts) if d]
    elif form == "halves":
        keep, send = parts
        came = exchange(send, 1)
        rows = keep.shape[0] // 2
        terms = [keep[:rows], came[:rows], exchange(keep[rows:] + came[rows:], 3)]
    else:
        keep, second, both, mirror = parts
        rows = keep.shape[0]
        came = exchange(both, 1)
        skip = lag_send(second, (0, 2), (3, 1))
        middle = lag_send(mirror, (1, 2), (2, 1))
        passed = lag_send(second + came[:rows], (1, 3), (2, 0))
        terms = [keep, came[rows:], skip, middle, passed]
    rows, lanes = terms[-1].shape
    return pl.pallas_call(
        turn_back_kernel,
        out_shape=jax.ShapeDtypeStruct((snaps, lanes // snaps, rows), jnp.float32),
        in_specs=[whole_vmem] * len(terms),
        out_specs=whole_vmem,
        compiler_params=pltpu.CompilerParams(vmem_limit_bytes=SMALL_BYTES),
        name="turn_back",
    )(*terms)


def local(image_grad, source_field, receiver_field):
    lag_count, depth, width = image_grad.shape
    snaps = source_field.shape[0]
    pad = lax.axis_size("lag") * lag_count // 2
    near, following, (receiver, source), (at_first, at_second) = gather_rows(
        image_grad, [receiver_field, source_field]
    )
    slabs = filter_slabs(image_grad, near, following, pad)
    first = sum_lags(1, FIRST_FORM, slabs, receiver, at_first, width)
    second = sum_lags(-1, SECOND_FORM, slabs, source, at_second, width, first[:1] if ORDERED else ())
    return sum_places(FIRST_FORM, first, snaps), sum_places(SECOND_FORM, second, snaps)


def solution(mesh):
    in_specs = (P("lag", "strip", None), P(None, None, "strip"), P(None, None, "strip"))
    out_specs = (P(None, "strip", "lag"), P(None, "strip", "lag"))
    return jax.shard_map(local, mesh=mesh, in_specs=in_specs, out_specs=out_specs, check_vma=False)
```

profile of v0, /device:TPU:0, one launch (start us, length us, event | category | flops | bytes accessed | tf_op | source)
XLA Modules:
  0.0 46.6 jit_solution(1654446698173203212)
XLA Ops:
  0.6 2.3 %send_rows.1 = (f32[1280,128]{1,0:T(8,128)S(1)}, f32[256,128]{1,0:T(8,128)S(1)}, f32[512,128]{1,0:T(8,128)S(1)}, f32[512,128]{1,0:T(8,128)S(1)}) custom-call(f32[32,64,1024]{2,1,0:T(8,128)} %grad_hbm.3, f32[2,512,128]{2,1,0:T(8,128)} %refs_0_.1, f32[2,512,128]{2,1,0:T(8,128)} %refs_1_.1), custom_call_target="tpu_custom_call" | custom-call | tf_op jit(solution)/shard_map/send_rows/pallas_call | solution.py:332
  2.9 0.5 %collective-permute-start = (f32[1280,128]{1,0:T(8,128)S(1)}, f32[1280,128]{1,0:T(8,128)S(1)}, u32[]{:S(2)}, u32[]{:S(2)}) collective-permute-start(f32[1280,128]{1,0:T(8,128)S(1)} %get-tuple-element.16), channel_id=1, source_target_pairs={{0,4},{4,0},{8,12},{12,8},{16,20},{20,16},{24,28},{28,24},{1,5},{5... | collective-permute-start | bytes 1966088 | tf_op jit(solution)/shard_map/ppermute | solution.py:317
  3.5 3.6 %collective-permute-start.1 = (f32[256,128]{1,0:T(8,128)S(1)}, f32[256,128]{1,0:T(8,128)S(1)}, u32[]{:S(2)}, u32[]{:S(2)}) collective-permute-start(f32[256,128]{1,0:T(8,128)S(1)} %get-tuple-element.17), channel_id=1, source_target_pairs={{4,8},{8,4},{12,16},{16,12},{20,24},{24,20},{28,0},{0,28},{5,9},{9... | collective-permute-start | bytes 393224 | tf_op jit(solution)/shard_map/ppermute | solution.py:344
  7.0 0.0 collective-permute-done.near_ref.refs_2_.refs_1_
  7.0 0.1 pack_fields.1
  7.1 1.1 %collective-permute-start.2 = (f32[512,128]{1,0:T(8,128)S(1)}, f32[512,128]{1,0:T(8,128)S(1)}, u32[]{:S(2)}, u32[]{:S(2)}) collective-permute-start(f32[512,128]{1,0:T(8,128)S(1)} %get-tuple-element.20), channel_id=1, source_target_pairs={{0,8},{4,12},{8,0},{12,4},{16,24},{20,28},{24,16},{28,20},{1,9},{5... | collective-permute-start | bytes 786440 | tf_op jit(solution)/shard_map/ppermute | solution.py:317
  8.2 1.5 %collective-permute-start.3 = (f32[512,128]{1,0:T(8,128)S(1)}, f32[512,128]{1,0:T(8,128)S(1)}, u32[]{:S(2)}, u32[]{:S(2)}) collective-permute-start(f32[512,128]{1,0:T(8,128)S(1)} %get-tuple-element.21), channel_id=1, source_target_pairs={{0,16},{4,20},{8,24},{12,28},{16,0},{20,4},{24,8},{28,12},{1,17},{... | collective-permute-start | bytes 786440 | tf_op jit(solution)/shard_map/ppermute | solution.py:317
  9.7 0.9 %collective-permute-start.4 = (f32[256,128]{1,0:T(8,128)S(1)}, f32[256,128]{1,0:T(8,128)S(1)}, u32[]{:S(2)}, u32[]{:S(2)}) collective-permute-start(f32[256,128]{1,0:T(8,128)S(1)} %get-tuple-element.22), channel_id=1, source_target_pairs={{0,24},{4,28},{8,16},{12,20},{16,8},{20,12},{24,0},{28,4},{1,25},{... | collective-permute-start | bytes 393224 | tf_op jit(solution)/shard_map/ppermute | solution.py:317
  10.6 2.0 %collective-permute-start.8 = (f32[256,128]{1,0:T(8,128)S(1)}, f32[256,128]{1,0:T(8,128)S(1)}, u32[]{:S(2)}, u32[]{:S(2)}) collective-permute-start(f32[256,128]{1,0:T(8,128)S(1)} %get-tuple-element.27), channel_id=1, source_target_pairs={{0,24},{4,28},{8,16},{12,20},{16,8},{20,12},{24,0},{28,4},{1,25},{... | collective-permute-start | bytes 393224 | tf_op jit(solution)/shard_map/ppermute | solution.py:317
  12.6 0.0 collective-permute-done.1.next_ref
  12.6 7.0 %filter_slabs.1.slab_ref = f32[16,1152,128]{2,1,0:T(8,128)S(1)} custom-call(f32[32,64,1024]{2,1,0:T(8,128)} %grad_hbm.3, f32[1280,128]{1,0:T(8,128)S(1)} %collective-permute-done.near_ref.refs_2_.refs_1_, f32[256,128]{1,0:T(8,128)S(1)} %collective-permute-done.1.next_ref), custom_call_target="tpu_custom_call" | custom-call | flops 3000000000 | bytes 3000000000 | tf_op jit(solution)/shard_map/filter_slabs/pallas_call | solution.py:128
  19.6 0.6 %collective-permute-done.4.refs_4_ = f32[256,128]{1,0:T(8,128)S(1)} collective-permute-done((f32[256,128]{1,0:T(8,128)S(1)}, f32[256,128]{1,0:T(8,128)S(1)}, u32[]{:S(2)}, u32[]{:S(2)}) %collective-permute-start.4) | collective-permute-done | bytes 131104 | tf_op jit(solution)/shard_map/ppermute | solution.py:317
  20.2 0.0 collective-permute-done.2.refs_2_
  20.2 0.7 %collective-permute-done.3.refs_3_ = f32[512,128]{1,0:T(8,128)S(1)} collective-permute-done((f32[512,128]{1,0:T(8,128)S(1)}, f32[512,128]{1,0:T(8,128)S(1)}, u32[]{:S(2)}, u32[]{:S(2)}) %collective-permute-start.3) | collective-permute-done | bytes 262176 | tf_op jit(solution)/shard_map/ppermute | solution.py:317
  20.9 1.9 %sum_lags.2 = (f32[256,128]{1,0:T(8,128)S(1)}, f32[256,128]{1,0:T(8,128)S(1)}, f32[256,128]{1,0:T(8,128)S(1)}, f32[256,128]{1,0:T(8,128)S(1)}) custom-call(f32[16,1152,128]{2,1,0:T(8,128)S(1)} %filter_slabs.1.slab_ref, f32[512,128]{1,0:T(8,128)S(1)} %get-tuple-element.18.refs_0_, f32[1280,128]{1,0:T(8,128)S(1)} %collective-permute-done.near_ref.refs_2_.refs_1_, ...), custom_call_target="tpu_custom_call" | custom-call | tf_op jit(solution)/shard_map/sum_lags/pallas_call | solution.py:244
  22.8 0.0 collective-permute-done.8.refs_4_
  22.8 2.2 %sum_lags.3 = (f32[512,128]{1,0:T(8,128)S(1)}, f32[512,128]{1,0:T(8,128)S(1)}) custom-call(f32[16,1152,128]{2,1,0:T(8,128)S(1)} %filter_slabs.1.slab_ref, f32[512,128]{1,0:T(8,128)S(1)} %get-tuple-element.19.refs_1_.refs_0_, f32[1280,128]{1,0:T(8,128)S(1)} %collective-permute-done.near_ref.refs_2_.refs_1_, f32[512,128]{1,0:T(8,128)S(1)} %collective-permute-done.2.refs_2_, ...), custom_call_target="tpu_custom_call" | custom-call | flops 1000000000 | bytes 1000000000 | tf_op jit(solution)/shard_map/sum_lags/pallas_call | solution.py:244
  25.0 1.3 %collective-permute-start.9 = (f32[512,128]{1,0:T(8,128)S(1)}, f32[512,128]{1,0:T(8,128)S(1)}, u32[]{:S(2)}, u32[]{:S(2)}) collective-permute-start(f32[512,128]{1,0:T(8,128)S(1)} %get-tuple-element.29), channel_id=1, source_target_pairs={{0,1},{1,0},{2,3},{3,2},{4,5},{5,4},{6,7},{7,6},{8,9},{9,8},{10,11... | collective-permute-start | bytes 786440 | tf_op jit(solution)/shard_map/ppermute | solution.py:381
  26.3 0.8 %collective-permute-start.5 = (f32[256,128]{1,0:T(8,128)S(1)}, f32[256,128]{1,0:T(8,128)S(1)}, u32[]{:S(2)}, u32[]{:S(2)}) collective-permute-start(f32[256,128]{1,0:T(8,128)S(1)} %get-tuple-element.24), channel_id=1, source_target_pairs={{0,1},{1,0},{2,3},{3,2},{4,5},{5,4},{6,7},{7,6},{8,9},{9,8},{10,11... | collective-permute-start | bytes 393224 | tf_op jit(solution)/shard_map/ppermute | solution.py:381
  27.1 2.3 %collective-permute-start.6 = (f32[256,128]{1,0:T(8,128)S(1)}, f32[256,128]{1,0:T(8,128)S(1)}, u32[]{:S(2)}, u32[]{:S(2)}) collective-permute-start(f32[256,128]{1,0:T(8,128)S(1)} %get-tuple-element.25), channel_id=1, source_target_pairs={{0,2},{1,3},{2,0},{3,1},{4,6},{5,7},{6,4},{7,5},{8,10},{9,11},{10,... | collective-permute-start | bytes 393224 | tf_op jit(solution)/shard_map/ppermute | solution.py:381
  29.4 1.3 %collective-permute-start.7 = (f32[256,128]{1,0:T(8,128)S(1)}, f32[256,128]{1,0:T(8,128)S(1)}, u32[]{:S(2)}, u32[]{:S(2)}) collective-permute-start(f32[256,128]{1,0:T(8,128)S(1)} %get-tuple-element.26), channel_id=1, source_target_pairs={{0,3},{1,2},{2,1},{3,0},{4,7},{5,6},{6,5},{7,4},{8,11},{9,10},{10,... | collective-permute-start | bytes 393224 | tf_op jit(solution)/shard_map/ppermute | solution.py:381
  30.7 5.8 %collective-permute-done.9 = f32[512,128]{1,0:T(8,128)S(1)} collective-permute-done((f32[512,128]{1,0:T(8,128)S(1)}, f32[512,128]{1,0:T(8,128)S(1)}, u32[]{:S(2)}, u32[]{:S(2)}) %collective-permute-start.9) | collective-permute-done | bytes 262176 | tf_op jit(solution)/shard_map/ppermute | solution.py:381
  36.6 4.1 %collective-permute-start.10 = (f32[256,128]{1,0:T(8,128)S(1)}, f32[256,128]{1,0:T(8,128)S(1)}, u32[]{:S(2)}, u32[]{:S(2)}) collective-permute-start(f32[256,128]{1,0:T(8,128)S(1)} %get-tuple-element.30), channel_id=1, source_target_pairs={{0,3},{1,2},{2,1},{3,0},{4,7},{5,6},{6,5},{7,4},{8,11},{9,10},{10,... | collective-permute-start | bytes 393224 | tf_op jit(solution)/shard_map/ppermute | solution.py:381
  40.6 0.0 collective-permute-done.5.refs_1_
  40.6 0.0 collective-permute-done.6.refs_2_
  40.7 3.8 %collective-permute-done.7.refs_3_ = f32[256,128]{1,0:T(8,128)S(1)} collective-permute-done((f32[256,128]{1,0:T(8,128)S(1)}, f32[256,128]{1,0:T(8,128)S(1)}, u32[]{:S(2)}, u32[]{:S(2)}) %collective-permute-start.7) | collective-permute-done | bytes 131104 | tf_op jit(solution)/shard_map/ppermute | solution.py:381
  44.4 0.8 %turn_back.2 = f32[2,64,256]{2,1,0:T(8,128)} custom-call(f32[256,128]{1,0:T(8,128)S(1)} %get-tuple-element.23.refs_0_.refs_5_, f32[256,128]{1,0:T(8,128)S(1)} %collective-permute-done.5.refs_1_, f32[256,128]{1,0:T(8,128)S(1)} %collective-permute-done.6.refs_2_, f32[256,128]{1,0:T(8,128)S(1)} %collective-permute-done.7.refs_3_), custom_call_target="tpu_custom_call" | custom-call | tf_op jit(solution)/shard_map/turn_back/pallas_call | solution.py:418
  45.2 0.6 %collective-permute-done.10.refs_2_ = f32[256,128]{1,0:T(8,128)S(1)} collective-permute-done((f32[256,128]{1,0:T(8,128)S(1)}, f32[256,128]{1,0:T(8,128)S(1)}, u32[]{:S(2)}, u32[]{:S(2)}) %collective-permute-start.10) | collective-permute-done | bytes 131104 | tf_op jit(solution)/shard_map/ppermute | solution.py:381
  45.8 0.8 %turn_back.3 = f32[2,64,256]{2,1,0:T(8,128)} custom-call(f32[256,128]{1,0:T(8,128)S(1)} %get-tuple-element.31.refs_0_, f32[256,128]{1,0:T(8,128)S(1)} %get-tuple-element.32.refs_1_, f32[256,128]{1,0:T(8,128)S(1)} %collective-permute-done.10.refs_2_), custom_call_target="tpu_custom_call" | custom-call | tf_op jit(solution)/shard_map/turn_back/pallas_call | solution.py:418
  (1 shorter events, 0.0 us)
Async XLA Ops:
  2.9 4.1 %collective-permute-start = (f32[1280,128]{1,0:T(8,128)S(1)}, f32[1280,128]{1,0:T(8,128)S(1)}, u32[]{:S(2)}, u32[]{:S(2)}) collective-permute-start(f32[1280,128]{1,0:T(8,128)S(1)} %get-tuple-element.16), channel_id=1, source_target_pairs={{0,4},{4,0},{8,12},{12,8},{16,20},{20,16},{24,28},{28,24},{1,5},{5... | collective-permute-start | bytes 1966088 | tf_op jit(solution)/shard_map/ppermute | solution.py:317
  3.5 9.2 %collective-permute-start.1 = (f32[256,128]{1,0:T(8,128)S(1)}, f32[256,128]{1,0:T(8,128)S(1)}, u32[]{:S(2)}, u32[]{:S(2)}) collective-permute-start(f32[256,128]{1,0:T(8,128)S(1)} %get-tuple-element.17), channel_id=1, source_target_pairs={{4,8},{8,4},{12,16},{16,12},{20,24},{24,20},{28,0},{0,28},{5,9},{9... | collective-permute-start | bytes 393224 | tf_op jit(solution)/shard_map/ppermute | solution.py:344
  7.1 13.1 %collective-permute-start.2 = (f32[512,128]{1,0:T(8,128)S(1)}, f32[512,128]{1,0:T(8,128)S(1)}, u32[]{:S(2)}, u32[]{:S(2)}) collective-permute-start(f32[512,128]{1,0:T(8,128)S(1)} %get-tuple-element.20), channel_id=1, source_target_pairs={{0,8},{4,12},{8,0},{12,4},{16,24},{20,28},{24,16},{28,20},{1,9},{5... | collective-permute-start | bytes 786440 | tf_op jit(solution)/shard_map/ppermute | solution.py:317
  8.2 12.8 %collective-permute-start.3 = (f32[512,128]{1,0:T(8,128)S(1)}, f32[512,128]{1,0:T(8,128)S(1)}, u32[]{:S(2)}, u32[]{:S(2)}) collective-permute-start(f32[512,128]{1,0:T(8,128)S(1)} %get-tuple-element.21), channel_id=1, source_target_pairs={{0,16},{4,20},{8,24},{12,28},{16,0},{20,4},{24,8},{28,12},{1,17},{... | collective-permute-start | bytes 786440 | tf_op jit(solution)/shard_map/ppermute | solution.py:317
  9.7 10.5 %collective-permute-start.4 = (f32[256,128]{1,0:T(8,128)S(1)}, f32[256,128]{1,0:T(8,128)S(1)}, u32[]{:S(2)}, u32[]{:S(2)}) collective-permute-start(f32[256,128]{1,0:T(8,128)S(1)} %get-tuple-element.22), channel_id=1, source_target_pairs={{0,24},{4,28},{8,16},{12,20},{16,8},{20,12},{24,0},{28,4},{1,25},{... | collective-permute-start | bytes 393224 | tf_op jit(solution)/shard_map/ppermute | solution.py:317
  10.6 12.1 %collective-permute-start.8 = (f32[256,128]{1,0:T(8,128)S(1)}, f32[256,128]{1,0:T(8,128)S(1)}, u32[]{:S(2)}, u32[]{:S(2)}) collective-permute-start(f32[256,128]{1,0:T(8,128)S(1)} %get-tuple-element.27), channel_id=1, source_target_pairs={{0,24},{4,28},{8,16},{12,20},{16,8},{20,12},{24,0},{28,4},{1,25},{... | collective-permute-start | bytes 393224 | tf_op jit(solution)/shard_map/ppermute | solution.py:317
  25.0 11.5 %collective-permute-start.9 = (f32[512,128]{1,0:T(8,128)S(1)}, f32[512,128]{1,0:T(8,128)S(1)}, u32[]{:S(2)}, u32[]{:S(2)}) collective-permute-start(f32[512,128]{1,0:T(8,128)S(1)} %get-tuple-element.29), channel_id=1, source_target_pairs={{0,1},{1,0},{2,3},{3,2},{4,5},{5,4},{6,7},{7,6},{8,9},{9,8},{10,11... | collective-permute-start | bytes 786440 | tf_op jit(solution)/shard_map/ppermute | solution.py:381
  26.3 14.3 %collective-permute-start.5 = (f32[256,128]{1,0:T(8,128)S(1)}, f32[256,128]{1,0:T(8,128)S(1)}, u32[]{:S(2)}, u32[]{:S(2)}) collective-permute-start(f32[256,128]{1,0:T(8,128)S(1)} %get-tuple-element.24), channel_id=1, source_target_pairs={{0,1},{1,0},{2,3},{3,2},{4,5},{5,4},{6,7},{7,6},{8,9},{9,8},{10,11... | collective-permute-start | bytes 393224 | tf_op jit(solution)/shard_map/ppermute | solution.py:381
  27.1 13.5 %collective-permute-start.6 = (f32[256,128]{1,0:T(8,128)S(1)}, f32[256,128]{1,0:T(8,128)S(1)}, u32[]{:S(2)}, u32[]{:S(2)}) collective-permute-start(f32[256,128]{1,0:T(8,128)S(1)} %get-tuple-element.25), channel_id=1, source_target_pairs={{0,2},{1,3},{2,0},{3,1},{4,6},{5,7},{6,4},{7,5},{8,10},{9,11},{10,... | collective-permute-start | bytes 393224 | tf_op jit(solution)/shard_map/ppermute | solution.py:381
  29.4 15.0 %collective-permute-start.7 = (f32[256,128]{1,0:T(8,128)S(1)}, f32[256,128]{1,0:T(8,128)S(1)}, u32[]{:S(2)}, u32[]{:S(2)}) collective-permute-start(f32[256,128]{1,0:T(8,128)S(1)} %get-tuple-element.26), channel_id=1, source_target_pairs={{0,3},{1,2},{2,1},{3,0},{4,7},{5,6},{6,5},{7,4},{8,11},{9,10},{10,... | collective-permute-start | bytes 393224 | tf_op jit(solution)/shard_map/ppermute | solution.py:381
  36.6 9.3 %collective-permute-start.10 = (f32[256,128]{1,0:T(8,128)S(1)}, f32[256,128]{1,0:T(8,128)S(1)}, u32[]{:S(2)}, u32[]{:S(2)}) collective-permute-start(f32[256,128]{1,0:T(8,128)S(1)} %get-tuple-element.30), channel_id=1, source_target_pairs={{0,3},{1,2},{2,1},{3,0},{4,7},{5,6},{6,5},{7,4},{8,11},{9,10},{10,... | collective-permute-start | bytes 393224 | tf_op jit(solution)/shard_map/ppermute | solution.py:381
where the time goes:
time: 46.7 us; the launch traced here: 46.6 us
  starting transfers between devices  19.4 us (42%)
  Pallas kernels  14.9 us (32%)
  waiting for transfers between devices  11.6 us (25%)
  between operations  0.68 us (1%)
    ppermute x5, waiting for transfers between devices, exchange(): return lax.ppermute(parts, 'lag', [(i, i ^ distance) for i in range(count)])  10.2 us
    ppermute x5, starting transfers between devices, exchange(): return lax.ppermute(parts, 'lag', [(i, i ^ distance) for i in range(count)])  9.79 us
    pallas_call x1, Pallas kernels, filter_slabs(): pl.pallas_call(functools.partial(filter_kernel, pad), out_shape=jax.Shape...  6.95 us
    ppermute x5, starting transfers between devices, strip_swap(): lax.ppermute(part, 'strip', [(i, i ^ distance) for i in range(count)])  6.05 us
    pallas_call x2, Pallas kernels, sum_lags(): pl.pallas_call(functools.partial(sum_kernel, sign, places, where_at, BLOC...  4.07 us
    ppermute x1, starting transfers between devices, gather_rows(): lax.ppermute(following, 'strip', [p for i in range(1, count, 2) for p in...  3.56 us
    pallas_call x1, Pallas kernels, gather_rows(): pl.pallas_call(functools.partial(send_kernel, pieces), out_shape=[buffer(...  2.3 us
    pallas_call x2, Pallas kernels, sum_places(): pl.pallas_call(turn_back_kernel, out_shape=jax.ShapeDtypeStruct((snaps, l...  1.53 us
  transfers between devices with their start and end apart: 11, of which 5 were waited for; matrix products, arithmetic and copies ran while one was open for 0% of the time, Pallas kernels for 21%

commit v1 on v0

--- a/solution.py
+++ b/solution.py
@@ -13,19 +13,21 @@
 PAIRS = 4
 CHUNK = 512
 ALONE = 1
-FIRST_FORM = "direct"
-SECOND_FORM = "halves"
+FIRST_FORM = "halves"
+SECOND_FORM = "direct"
 ORDERED = True
 GRAD_IN_HBM = True
 FILTER_COST = 3 * 10**9
 FIRST_COST = 0
 SECOND_COST = 10**9
+BACK_COST = 5 * 10**10
+CHAIN = True
 FILTER_BYTES = 32 * 1024 * 1024
 SUM_BYTES = 8 * 1024 * 1024
 SMALL_BYTES = 4 * 1024 * 1024
 
 def weight(size):
-    return pl.CostEstimate(flops=size, bytes_accessed=size, transcendentals=0)
+    return pl.CostEstimate(flops=size, bytes_accessed=min(size, 10**7), transcendentals=0)
 
 
 def in_hbm(array):
@@ -272,7 +274,7 @@
         copies.append(pltpu.make_async_copy(grad_hbm.at[:, rows], edges.at[side], sems.at[side]))
     for f in range(number):
         copies.append(pltpu.make_async_copy(fields[f], held[f], sems.at[2 + f]))
-    for copy in copies:
+    for copy in copies[2:] + copies[:2]:
         copy.start()
 
     for f in range(number):
@@ -394,18 +396,31 @@
             out_ref[snap, :, rows] = turned[snap * depth : (snap + 1) * depth]
 
 
+def add_kernel(keep_ref, came_ref, *refs):
+    rows = refs[-1].shape[0]
+    refs[-1][...] = keep_ref[pl.ds(rows, rows)] + came_ref[pl.ds(rows, rows)]
+
+
 def lag_send(part, *pairs):
     return lax.ppermute(part, "lag", pairs)
 
 
-def sum_places(form, parts, snaps):
+def sum_places(form, parts, snaps, after=()):
     if form == "direct":
         terms = [parts[0]] + [exchange(part, d) for d, part in enumerate(parts) if d]
     elif form == "halves":
         keep, send = parts
         came = exchange(send, 1)
         rows = keep.shape[0] // 2
-        terms = [keep[:rows], came[:rows], exchange(keep[rows:] + came[rows:], 3)]
+        passed = pl.pallas_call(
+            add_kernel,
+            out_shape=jax.ShapeDtypeStruct((rows, keep.shape[1]), jnp.float32),
+            in_specs=[whole_vmem] * 2 + [pl.BlockSpec(memory_space=pltpu.HBM)] * len(after),
+            out_specs=whole_vmem,
+            compiler_params=pltpu.CompilerParams(vmem_limit_bytes=SMALL_BYTES),
+            name="add_mirror",
+        )(keep, came, *(in_hbm(a) for a in after))
+        terms = [keep, came, exchange(passed, 3)]
     else:
         keep, second, both, mirror = parts
         rows = keep.shape[0]
@@ -421,6 +436,7 @@
         in_specs=[whole_vmem] * len(terms),
         out_specs=whole_vmem,
         compiler_params=pltpu.CompilerParams(vmem_limit_bytes=SMALL_BYTES),
+        cost_estimate=weight(BACK_COST),
         name="turn_back",
     )(*terms)
 
@@ -435,7 +451,9 @@
     slabs = filter_slabs(image_grad, near, following, pad)
     first = sum_lags(1, FIRST_FORM, slabs, receiver, at_first, width)
     second = sum_lags(-1, SECOND_FORM, slabs, source, at_second, width, first[:1] if ORDERED else ())
-    return sum_places(FIRST_FORM, first, snaps), sum_places(SECOND_FORM, second, snaps)
+    source_adjoint = sum_places(FIRST_FORM, first, snaps)
+    receiver_adjoint = sum_places(SECOND_FORM, second, snaps, (source_adjoint,) if CHAIN else ())
+    return source_adjoint, receiver_adjoint
 
 
 def solution(mesh):

time: 46.7 us -> 45 us (0.964); the launches traced: 46.6 us -> 44.1 us
  waiting for transfers between devices: 11.6 us -> 9.96 us
  starting transfers between devices: 19.4 us -> 18.8 us
    ppermute x5, waiting for transfers between devices: 10.2 us -> 8.61 us  [exchange(): return lax.ppermute(parts, 'lag', [(i, i ^ distance) for i in range(count)])]
    ppermute x5, starting transfers between devices: 9.79 us -> 9.2 us  [exchange(): return lax.ppermute(parts, 'lag', [(i, i ^ distance) for i in range(count)])]
  transfers between devices with their start and end apart: 11 -> 11, of which waited for: 5 -> 4; matrix products, arithmetic and copies ran while one was open for 0% -> 0% of each run, Pallas kernels for 21% -> 27%
where the time goes in v1:
time: 45 us; the launch traced here: 44.1 us
  starting transfers between devices  18.8 us (42%)
  Pallas kernels  14.7 us (33%)
  waiting for transfers between devices  9.96 us (22%)
  between operations  0.67 us (1%)
    ppermute x5, starting transfers between devices, exchange(): return lax.ppermute(parts, 'lag', [(i, i ^ distance) for i in range(count)])  9.2 us
    ppermute x5, waiting for transfers between devices, exchange(): return lax.ppermute(parts, 'lag', [(i, i ^ distance) for i in range(count)])  8.61 us
    pallas_call x1, Pallas kernels, filter_slabs(): pl.pallas_call(functools.partial(filter_kernel, pad), out_shape=jax.Shape...  6.96 us
    ppermute x5, starting transfers between devices, strip_swap(): lax.ppermute(part, 'strip', [(i, i ^ distance) for i in range(count)])  6.05 us
    pallas_call x2, Pallas kernels, sum_lags(): pl.pallas_call(functools.partial(sum_kernel, sign, places, where_at, BLOC...  4.07 us
    ppermute x1, starting transfers between devices, gather_rows(): lax.ppermute(following, 'strip', [p for i in range(1, count, 2) for p in...  3.56 us
    pallas_call x1, Pallas kernels, gather_rows(): pl.pallas_call(functools.partial(send_kernel, pieces), out_shape=[buffer(...  2.08 us
    pallas_call x2, Pallas kernels, sum_places(): pl.pallas_call(turn_back_kernel, out_shape=jax.ShapeDtypeStruct((snaps, l...  1.52 us
  transfers between devices with their start and end apart: 11, of which 4 were waited for; matrix products, arithmetic and copies ran while one was open for 0% of the time, Pallas kernels for 27%

profile of v1, /device:TPU:0, one launch (start us, length us, event | category | flops | bytes accessed | tf_op | source)
XLA Modules:
  0.0 44.1 jit_solution(5527268553938061136)
XLA Ops:
  0.6 2.1 %send_rows.1 = (f32[1280,128]{1,0:T(8,128)S(1)}, f32[256,128]{1,0:T(8,128)S(1)}, f32[512,128]{1,0:T(8,128)S(1)}, f32[512,128]{1,0:T(8,128)S(1)}) custom-call(f32[32,64,1024]{2,1,0:T(8,128)} %grad_hbm.3, f32[2,512,128]{2,1,0:T(8,128)} %refs_0_.1, f32[2,512,128]{2,1,0:T(8,128)} %refs_1_.1), custom_call_target="tpu_custom_call" | custom-call | tf_op jit(solution)/shard_map/send_rows/pallas_call | solution.py:334
  2.7 0.5 %collective-permute-start = (f32[1280,128]{1,0:T(8,128)S(1)}, f32[1280,128]{1,0:T(8,128)S(1)}, u32[]{:S(2)}, u32[]{:S(2)}) collective-permute-start(f32[1280,128]{1,0:T(8,128)S(1)} %get-tuple-element.16), channel_id=1, source_target_pairs={{0,4},{4,0},{8,12},{12,8},{16,20},{20,16},{24,28},{28,24},{1,5},{5... | collective-permute-start | bytes 1966088 | tf_op jit(solution)/shard_map/ppermute | solution.py:319
  3.2 3.6 %collective-permute-start.1 = (f32[256,128]{1,0:T(8,128)S(1)}, f32[256,128]{1,0:T(8,128)S(1)}, u32[]{:S(2)}, u32[]{:S(2)}) collective-permute-start(f32[256,128]{1,0:T(8,128)S(1)} %get-tuple-element.17), channel_id=1, source_target_pairs={{4,8},{8,4},{12,16},{16,12},{20,24},{24,20},{28,0},{0,28},{5,9},{9... | collective-permute-start | bytes 393224 | tf_op jit(solution)/shard_map/ppermute | solution.py:346
  6.8 0.0 collective-permute-done.near_ref.refs_2_.refs_1_
  6.8 0.1 pack_fields.1
  6.9 1.1 %collective-permute-start.2 = (f32[512,128]{1,0:T(8,128)S(1)}, f32[512,128]{1,0:T(8,128)S(1)}, u32[]{:S(2)}, u32[]{:S(2)}) collective-permute-start(f32[512,128]{1,0:T(8,128)S(1)} %get-tuple-element.20), channel_id=1, source_target_pairs={{0,8},{4,12},{8,0},{12,4},{16,24},{20,28},{24,16},{28,20},{1,9},{5... | collective-permute-start | bytes 786440 | tf_op jit(solution)/shard_map/ppermute | solution.py:319
  7.9 1.5 %collective-permute-start.3 = (f32[512,128]{1,0:T(8,128)S(1)}, f32[512,128]{1,0:T(8,128)S(1)}, u32[]{:S(2)}, u32[]{:S(2)}) collective-permute-start(f32[512,128]{1,0:T(8,128)S(1)} %get-tuple-element.21), channel_id=1, source_target_pairs={{0,16},{4,20},{8,24},{12,28},{16,0},{20,4},{24,8},{28,12},{1,17},{... | collective-permute-start | bytes 786440 | tf_op jit(solution)/shard_map/ppermute | solution.py:319
  9.5 0.9 %collective-permute-start.4 = (f32[256,128]{1,0:T(8,128)S(1)}, f32[256,128]{1,0:T(8,128)S(1)}, u32[]{:S(2)}, u32[]{:S(2)}) collective-permute-start(f32[256,128]{1,0:T(8,128)S(1)} %get-tuple-element.22), channel_id=1, source_target_pairs={{0,24},{4,28},{8,16},{12,20},{16,8},{20,12},{24,0},{28,4},{1,25},{... | collective-permute-start | bytes 393224 | tf_op jit(solution)/shard_map/ppermute | solution.py:319
  10.4 2.0 %collective-permute-start.7 = (f32[256,128]{1,0:T(8,128)S(1)}, f32[256,128]{1,0:T(8,128)S(1)}, u32[]{:S(2)}, u32[]{:S(2)}) collective-permute-start(f32[256,128]{1,0:T(8,128)S(1)} %get-tuple-element.25), channel_id=1, source_target_pairs={{0,24},{4,28},{8,16},{12,20},{16,8},{20,12},{24,0},{28,4},{1,25},{... | collective-permute-start | bytes 393224 | tf_op jit(solution)/shard_map/ppermute | solution.py:319
  12.4 0.0 collective-permute-done.1.next_ref
  12.4 7.0 %filter_slabs.1.slab_ref = f32[16,1152,128]{2,1,0:T(8,128)S(1)} custom-call(f32[32,64,1024]{2,1,0:T(8,128)} %grad_hbm.3, f32[1280,128]{1,0:T(8,128)S(1)} %collective-permute-done.near_ref.refs_2_.refs_1_, f32[256,128]{1,0:T(8,128)S(1)} %collective-permute-done.1.next_ref), custom_call_target="tpu_custom_call" | custom-call | flops 3000000000 | bytes 10000000 | tf_op jit(solution)/shard_map/filter_slabs/pallas_call | solution.py:130
  19.4 0.6 %collective-permute-done.4.refs_4_ = f32[256,128]{1,0:T(8,128)S(1)} collective-permute-done((f32[256,128]{1,0:T(8,128)S(1)}, f32[256,128]{1,0:T(8,128)S(1)}, u32[]{:S(2)}, u32[]{:S(2)}) %collective-permute-start.4) | collective-permute-done | bytes 131104 | tf_op jit(solution)/shard_map/ppermute | solution.py:319
  19.9 0.0 collective-permute-done.2.refs_2_
  20.0 0.7 %collective-permute-done.3.refs_3_ = f32[512,128]{1,0:T(8,128)S(1)} collective-permute-done((f32[512,128]{1,0:T(8,128)S(1)}, f32[512,128]{1,0:T(8,128)S(1)}, u32[]{:S(2)}, u32[]{:S(2)}) %collective-permute-start.3) | collective-permute-done | bytes 262176 | tf_op jit(solution)/shard_map/ppermute | solution.py:319
  20.7 1.9 %sum_lags.2 = (f32[512,128]{1,0:T(8,128)S(1)}, f32[512,128]{1,0:T(8,128)S(1)}) custom-call(f32[16,1152,128]{2,1,0:T(8,128)S(1)} %filter_slabs.1.slab_ref, f32[512,128]{1,0:T(8,128)S(1)} %get-tuple-element.18.refs_0_, f32[1280,128]{1,0:T(8,128)S(1)} %collective-permute-done.near_ref.refs_2_.refs_1_, f32[512,128]{1,0:T(8,128)S(1)} %collective-permute-done.2.refs_2_, ...), custom_call_target="tpu_custom_call" | custom-call | tf_op jit(solution)/shard_map/sum_lags/pallas_call | solution.py:246
  22.6 1.0 %collective-permute-start.5 = (f32[512,128]{1,0:T(8,128)S(1)}, f32[512,128]{1,0:T(8,128)S(1)}, u32[]{:S(2)}, u32[]{:S(2)}) collective-permute-start(f32[512,128]{1,0:T(8,128)S(1)} %get-tuple-element.24), channel_id=1, source_target_pairs={{0,1},{1,0},{2,3},{3,2},{4,5},{5,4},{6,7},{7,6},{8,9},{9,8},{10,11... | collective-permute-start | bytes 786440 | tf_op jit(solution)/shard_map/ppermute | solution.py:383
  23.6 0.0 collective-permute-done.7.refs_4_
  23.6 2.2 %sum_lags.3 = (f32[256,128]{1,0:T(8,128)S(1)}, f32[256,128]{1,0:T(8,128)S(1)}, f32[256,128]{1,0:T(8,128)S(1)}, f32[256,128]{1,0:T(8,128)S(1)}) custom-call(f32[16,1152,128]{2,1,0:T(8,128)S(1)} %filter_slabs.1.slab_ref, f32[512,128]{1,0:T(8,128)S(1)} %get-tuple-element.19.refs_1_.refs_0_, f32[1280,128]{1,0:T(8,128)S(1)} %collective-permute-done.near_ref.refs_2_.refs_1_, ...), custom_call_target="tpu_custom_call" | custom-call | flops 1000000000 | bytes 10000000 | tf_op jit(solution)/shard_map/sum_lags/pallas_call | solution.py:246
  25.8 1.2 %collective-permute-start.8 = (f32[256,128]{1,0:T(8,128)S(1)}, f32[256,128]{1,0:T(8,128)S(1)}, u32[]{:S(2)}, u32[]{:S(2)}) collective-permute-start(f32[256,128]{1,0:T(8,128)S(1)} %get-tuple-element.27), channel_id=1, source_target_pairs={{0,1},{1,0},{2,3},{3,2},{4,5},{5,4},{6,7},{7,6},{8,9},{9,8},{10,11... | collective-permute-start | bytes 393224 | tf_op jit(solution)/shard_map/ppermute | solution.py:383
  26.9 1.9 %collective-permute-start.9 = (f32[256,128]{1,0:T(8,128)S(1)}, f32[256,128]{1,0:T(8,128)S(1)}, u32[]{:S(2)}, u32[]{:S(2)}) collective-permute-start(f32[256,128]{1,0:T(8,128)S(1)} %get-tuple-element.28), channel_id=1, source_target_pairs={{0,2},{1,3},{2,0},{3,1},{4,6},{5,7},{6,4},{7,5},{8,10},{9,11},{10,... | collective-permute-start | bytes 393224 | tf_op jit(solution)/shard_map/ppermute | solution.py:383
  28.9 1.3 %collective-permute-start.10 = (f32[256,128]{1,0:T(8,128)S(1)}, f32[256,128]{1,0:T(8,128)S(1)}, u32[]{:S(2)}, u32[]{:S(2)}) collective-permute-start(f32[256,128]{1,0:T(8,128)S(1)} %get-tuple-element.29), channel_id=1, source_target_pairs={{0,3},{1,2},{2,1},{3,0},{4,7},{5,6},{6,5},{7,4},{8,11},{9,10},{10,... | collective-permute-start | bytes 393224 | tf_op jit(solution)/shard_map/ppermute | solution.py:383
  30.2 1.9 %collective-permute-done.5.came_ref.refs_1_ = f32[512,128]{1,0:T(8,128)S(1)} collective-permute-done((f32[512,128]{1,0:T(8,128)S(1)}, f32[512,128]{1,0:T(8,128)S(1)}, u32[]{:S(2)}, u32[]{:S(2)}) %collective-permute-start.5) | collective-permute-done | bytes 262176 | tf_op jit(solution)/shard_map/ppermute | solution.py:383
  32.1 3.8 %collective-permute-start.6 = (f32[256,128]{1,0:T(8,128)S(1)}, f32[256,128]{1,0:T(8,128)S(1)}, u32[]{:S(2)}, u32[]{:S(2)}) collective-permute-start(f32[256,128]{1,0:T(8,128)S(1)} %add_mirror.1), channel_id=1, source_target_pairs={{0,3},{1,2},{2,1},{3,0},{4,7},{5,6},{6,5},{7,4},{8,11},{9,10},{10,... | collective-permute-start | bytes 393224 | tf_op jit(solution)/shard_map/ppermute | solution.py:383
  35.9 0.0 collective-permute-done.8.refs_1_
  35.9 6.7 %collective-permute-done.9.refs_2_ = f32[256,128]{1,0:T(8,128)S(1)} collective-permute-done((f32[256,128]{1,0:T(8,128)S(1)}, f32[256,128]{1,0:T(8,128)S(1)}, u32[]{:S(2)}, u32[]{:S(2)}) %collective-permute-start.9) | collective-permute-done | bytes 131104 | tf_op jit(solution)/shard_map/ppermute | solution.py:383
  42.6 0.0 collective-permute-done.10.refs_3_
  42.6 0.8 %turn_back.3 = f32[2,64,256]{2,1,0:T(8,128)} custom-call(f32[256,128]{1,0:T(8,128)S(1)} %get-tuple-element.26.refs_0_, f32[256,128]{1,0:T(8,128)S(1)} %collective-permute-done.8.refs_1_, f32[256,128]{1,0:T(8,128)S(1)} %collective-permute-done.9.refs_2_, f32[256,128]{1,0:T(8,128)S(1)} %collective-permute-done.10.refs_3_), custom_call_target="tpu_custom_call" | custom-call | flops 49999998976 | bytes 10000000 | tf_op jit(solution)/shard_map/turn_back/pallas_call | solution.py:433
  43.4 0.0 collective-permute-done.6.refs_2_
  43.4 0.8 %turn_back.2 = f32[2,64,256]{2,1,0:T(8,128)} custom-call(f32[512,128]{1,0:T(8,128)S(1)} %get-tuple-element.23.keep_ref.refs_0_.refs_5_, f32[512,128]{1,0:T(8,128)S(1)} %collective-permute-done.5.came_ref.refs_1_, f32[256,128]{1,0:T(8,128)S(1)} %collective-permute-done.6.refs_2_), custom_call_target="tpu_custom_call" | custom-call | flops 49999998976 | bytes 10000000 | tf_op jit(solution)/shard_map/turn_back/pallas_call | solution.py:433
  (1 shorter events, 0.0 us)
Async XLA Ops:
  2.7 4.1 %collective-permute-start = (f32[1280,128]{1,0:T(8,128)S(1)}, f32[1280,128]{1,0:T(8,128)S(1)}, u32[]{:S(2)}, u32[]{:S(2)}) collective-permute-start(f32[1280,128]{1,0:T(8,128)S(1)} %get-tuple-element.16), channel_id=1, source_target_pairs={{0,4},{4,0},{8,12},{12,8},{16,20},{20,16},{24,28},{28,24},{1,5},{5... | collective-permute-start | bytes 1966088 | tf_op jit(solution)/shard_map/ppermute | solution.py:319
  3.2 9.2 %collective-permute-start.1 = (f32[256,128]{1,0:T(8,128)S(1)}, f32[256,128]{1,0:T(8,128)S(1)}, u32[]{:S(2)}, u32[]{:S(2)}) collective-permute-start(f32[256,128]{1,0:T(8,128)S(1)} %get-tuple-element.17), channel_id=1, source_target_pairs={{4,8},{8,4},{12,16},{16,12},{20,24},{24,20},{28,0},{0,28},{5,9},{9... | collective-permute-start | bytes 393224 | tf_op jit(solution)/shard_map/ppermute | solution.py:346
  6.9 13.1 %collective-permute-start.2 = (f32[512,128]{1,0:T(8,128)S(1)}, f32[512,128]{1,0:T(8,128)S(1)}, u32[]{:S(2)}, u32[]{:S(2)}) collective-permute-start(f32[512,128]{1,0:T(8,128)S(1)} %get-tuple-element.20), channel_id=1, source_target_pairs={{0,8},{4,12},{8,0},{12,4},{16,24},{20,28},{24,16},{28,20},{1,9},{5... | collective-permute-start | bytes 786440 | tf_op jit(solution)/shard_map/ppermute | solution.py:319
  7.9 12.8 %collective-permute-start.3 = (f32[512,128]{1,0:T(8,128)S(1)}, f32[512,128]{1,0:T(8,128)S(1)}, u32[]{:S(2)}, u32[]{:S(2)}) collective-permute-start(f32[512,128]{1,0:T(8,128)S(1)} %get-tuple-element.21), channel_id=1, source_target_pairs={{0,16},{4,20},{8,24},{12,28},{16,0},{20,4},{24,8},{28,12},{1,17},{... | collective-permute-start | bytes 786440 | tf_op jit(solution)/shard_map/ppermute | solution.py:319
  9.5 10.5 %collective-permute-start.4 = (f32[256,128]{1,0:T(8,128)S(1)}, f32[256,128]{1,0:T(8,128)S(1)}, u32[]{:S(2)}, u32[]{:S(2)}) collective-permute-start(f32[256,128]{1,0:T(8,128)S(1)} %get-tuple-element.22), channel_id=1, source_target_pairs={{0,24},{4,28},{8,16},{12,20},{16,8},{20,12},{24,0},{28,4},{1,25},{... | collective-permute-start | bytes 393224 | tf_op jit(solution)/shard_map/ppermute | solution.py:319
  10.4 13.1 %collective-permute-start.7 = (f32[256,128]{1,0:T(8,128)S(1)}, f32[256,128]{1,0:T(8,128)S(1)}, u32[]{:S(2)}, u32[]{:S(2)}) collective-permute-start(f32[256,128]{1,0:T(8,128)S(1)} %get-tuple-element.25), channel_id=1, source_target_pairs={{0,24},{4,28},{8,16},{12,20},{16,8},{20,12},{24,0},{28,4},{1,25},{... | collective-permute-start | bytes 393224 | tf_op jit(solution)/shard_map/ppermute | solution.py:319
  22.6 9.6 %collective-permute-start.5 = (f32[512,128]{1,0:T(8,128)S(1)}, f32[512,128]{1,0:T(8,128)S(1)}, u32[]{:S(2)}, u32[]{:S(2)}) collective-permute-start(f32[512,128]{1,0:T(8,128)S(1)} %get-tuple-element.24), channel_id=1, source_target_pairs={{0,1},{1,0},{2,3},{3,2},{4,5},{5,4},{6,7},{7,6},{8,9},{9,8},{10,11... | collective-permute-start | bytes 786440 | tf_op jit(solution)/shard_map/ppermute | solution.py:383
  25.8 10.1 %collective-permute-start.8 = (f32[256,128]{1,0:T(8,128)S(1)}, f32[256,128]{1,0:T(8,128)S(1)}, u32[]{:S(2)}, u32[]{:S(2)}) collective-permute-start(f32[256,128]{1,0:T(8,128)S(1)} %get-tuple-element.27), channel_id=1, source_target_pairs={{0,1},{1,0},{2,3},{3,2},{4,5},{5,4},{6,7},{7,6},{8,9},{9,8},{10,11... | collective-permute-start | bytes 393224 | tf_op jit(solution)/shard_map/ppermute | solution.py:383
  26.9 15.7 %collective-permute-start.9 = (f32[256,128]{1,0:T(8,128)S(1)}, f32[256,128]{1,0:T(8,128)S(1)}, u32[]{:S(2)}, u32[]{:S(2)}) collective-permute-start(f32[256,128]{1,0:T(8,128)S(1)} %get-tuple-element.28), channel_id=1, source_target_pairs={{0,2},{1,3},{2,0},{3,1},{4,6},{5,7},{6,4},{7,5},{8,10},{9,11},{10,... | collective-permute-start | bytes 393224 | tf_op jit(solution)/shard_map/ppermute | solution.py:383
  28.9 13.7 %collective-permute-start.10 = (f32[256,128]{1,0:T(8,128)S(1)}, f32[256,128]{1,0:T(8,128)S(1)}, u32[]{:S(2)}, u32[]{:S(2)}) collective-permute-start(f32[256,128]{1,0:T(8,128)S(1)} %get-tuple-element.29), channel_id=1, source_target_pairs={{0,3},{1,2},{2,1},{3,0},{4,7},{5,6},{6,5},{7,4},{8,11},{9,10},{10,... | collective-permute-start | bytes 393224 | tf_op jit(solution)/shard_map/ppermute | solution.py:383
  32.1 11.2 %collective-permute-start.6 = (f32[256,128]{1,0:T(8,128)S(1)}, f32[256,128]{1,0:T(8,128)S(1)}, u32[]{:S(2)}, u32[]{:S(2)}) collective-permute-start(f32[256,128]{1,0:T(8,128)S(1)} %add_mirror.1), channel_id=1, source_target_pairs={{0,3},{1,2},{2,1},{3,0},{4,7},{5,6},{6,5},{7,4},{8,11},{9,10},{10,... | collective-permute-start | bytes 393224 | tf_op jit(solution)/shard_map/ppermute | solution.py:383

commit v2 on v1

--- a/solution.py
+++ b/solution.py
@@ -22,6 +22,7 @@
 SECOND_COST = 10**9
 BACK_COST = 5 * 10**10
 CHAIN = True
+DIRECT_ORDER = (2, 3, 1)
 FILTER_BYTES = 32 * 1024 * 1024
 SUM_BYTES = 8 * 1024 * 1024
 SMALL_BYTES = 4 * 1024 * 1024
@@ -407,7 +408,7 @@
 
 def sum_places(form, parts, snaps, after=()):
     if form == "direct":
-        terms = [parts[0]] + [exchange(part, d) for d, part in enumerate(parts) if d]
+        terms = [parts[0]] + [exchange(parts[d], d) for d in DIRECT_ORDER]
     elif form == "halves":
         keep, send = parts
         came = exchange(send, 1)

time: 45 us -> 44.2 us (0.982)
  the two profiles are of different devices: /device:TPU:0 before, /device:TPU:18 now
where the time goes in v2:
time: 44.2 us; the launch traced here: 44 us
  waiting for transfers between devices  16.7 us (38%)
  Pallas kernels  14.7 us (33%)
  starting transfers between devices  11.9 us (27%)
  between operations  0.69 us (2%)
    ppermute x5, waiting for transfers between devices, exchange(): return lax.ppermute(parts, 'lag', [(i, i ^ distance) for i in range(count)])  13.7 us
    pallas_call x1, Pallas kernels, filter_slabs(): pl.pallas_call(functools.partial(filter_kernel, pad), out_shape=jax.Shape...  6.96 us
    ppermute x5, starting transfers between devices, exchange(): return lax.ppermute(parts, 'lag', [(i, i ^ distance) for i in range(count)])  6.17 us
    ppermute x5, starting transfers between devices, strip_swap(): lax.ppermute(part, 'strip', [(i, i ^ distance) for i in range(count)])  5.12 us
    pallas_call x2, Pallas kernels, sum_lags(): pl.pallas_call(functools.partial(sum_kernel, sign, places, where_at, BLOC...  4.07 us
    ppermute x5, waiting for transfers between devices, strip_swap(): lax.ppermute(part, 'strip', [(i, i ^ distance) for i in range(count)])  3.03 us
    pallas_call x1, Pallas kernels, gather_rows(): pl.pallas_call(functools.partial(send_kernel, pieces), out_shape=[buffer(...  2.08 us
    pallas_call x2, Pallas kernels, sum_places(): pl.pallas_call(turn_back_kernel, out_shape=jax.ShapeDtypeStruct((snaps, l...  1.52 us
  transfers between devices with their start and end apart: 11, of which 6 were waited for; matrix products, arithmetic and copies ran while one was open for 0% of the time, Pallas kernels for 27%

profile of v2, /device:TPU:18, one launch (start us, length us, event | category | flops | bytes accessed | tf_op | source)
XLA Modules:
  0.0 44.0 jit_solution(8112954277938016460)
XLA Ops:
  0.6 2.1 %send_rows.1 = (f32[1280,128]{1,0:T(8,128)S(1)}, f32[256,128]{1,0:T(8,128)S(1)}, f32[512,128]{1,0:T(8,128)S(1)}, f32[512,128]{1,0:T(8,128)S(1)}) custom-call(f32[32,64,1024]{2,1,0:T(8,128)} %grad_hbm.3, f32[2,512,128]{2,1,0:T(8,128)} %refs_0_.1, f32[2,512,128]{2,1,0:T(8,128)} %refs_1_.1), custom_call_target="tpu_custom_call" | custom-call | tf_op jit(solution)/shard_map/send_rows/pallas_call | solution.py:335
  2.7 0.1 collective-permute-start
  2.8 0.6 %collective-permute-start.1 = (f32[256,128]{1,0:T(8,128)S(1)}, f32[256,128]{1,0:T(8,128)S(1)}, u32[]{:S(2)}, u32[]{:S(2)}) collective-permute-start(f32[256,128]{1,0:T(8,128)S(1)} %get-tuple-element.17), channel_id=1, source_target_pairs={{4,8},{8,4},{12,16},{16,12},{20,24},{24,20},{28,0},{0,28},{5,9},{9... | collective-permute-start | bytes 393224 | tf_op jit(solution)/shard_map/ppermute | solution.py:347
  3.4 1.4 %collective-permute-done.near_ref.refs_2_.refs_1_ = f32[1280,128]{1,0:T(8,128)S(1)} collective-permute-done((f32[1280,128]{1,0:T(8,128)S(1)}, f32[1280,128]{1,0:T(8,128)S(1)}, u32[]{:S(2)}, u32[]{:S(2)}) %collective-permute-start) | collective-permute-done | bytes 655392 | tf_op jit(solution)/shard_map/ppermute | solution.py:320
  4.9 0.1 pack_fields.1
  4.9 1.1 %collective-permute-start.2 = (f32[512,128]{1,0:T(8,128)S(1)}, f32[512,128]{1,0:T(8,128)S(1)}, u32[]{:S(2)}, u32[]{:S(2)}) collective-permute-start(f32[512,128]{1,0:T(8,128)S(1)} %get-tuple-element.20), channel_id=1, source_target_pairs={{0,8},{4,12},{8,0},{12,4},{16,24},{20,28},{24,16},{28,20},{1,9},{5... | collective-permute-start | bytes 786440 | tf_op jit(solution)/shard_map/ppermute | solution.py:320
  6.0 1.1 %collective-permute-start.3 = (f32[512,128]{1,0:T(8,128)S(1)}, f32[512,128]{1,0:T(8,128)S(1)}, u32[]{:S(2)}, u32[]{:S(2)}) collective-permute-start(f32[512,128]{1,0:T(8,128)S(1)} %get-tuple-element.21), channel_id=1, source_target_pairs={{0,16},{4,20},{8,24},{12,28},{16,0},{20,4},{24,8},{28,12},{1,17},{... | collective-permute-start | bytes 786440 | tf_op jit(solution)/shard_map/ppermute | solution.py:320
  7.1 1.4 %collective-permute-start.4 = (f32[256,128]{1,0:T(8,128)S(1)}, f32[256,128]{1,0:T(8,128)S(1)}, u32[]{:S(2)}, u32[]{:S(2)}) collective-permute-start(f32[256,128]{1,0:T(8,128)S(1)} %get-tuple-element.22), channel_id=1, source_target_pairs={{0,24},{4,28},{8,16},{12,20},{16,8},{20,12},{24,0},{28,4},{1,25},{... | collective-permute-start | bytes 393224 | tf_op jit(solution)/shard_map/ppermute | solution.py:320
  8.5 1.5 %collective-permute-start.7 = (f32[256,128]{1,0:T(8,128)S(1)}, f32[256,128]{1,0:T(8,128)S(1)}, u32[]{:S(2)}, u32[]{:S(2)}) collective-permute-start(f32[256,128]{1,0:T(8,128)S(1)} %get-tuple-element.25), channel_id=1, source_target_pairs={{0,24},{4,28},{8,16},{12,20},{16,8},{20,12},{24,0},{28,4},{1,25},{... | collective-permute-start | bytes 393224 | tf_op jit(solution)/shard_map/ppermute | solution.py:320
  10.0 0.0 collective-permute-done.1.next_ref
  10.0 7.0 %filter_slabs.1.slab_ref = f32[16,1152,128]{2,1,0:T(8,128)S(1)} custom-call(f32[32,64,1024]{2,1,0:T(8,128)} %grad_hbm.3, f32[1280,128]{1,0:T(8,128)S(1)} %collective-permute-done.near_ref.refs_2_.refs_1_, f32[256,128]{1,0:T(8,128)S(1)} %collective-permute-done.1.next_ref), custom_call_target="tpu_custom_call" | custom-call | flops 3000000000 | bytes 10000000 | tf_op jit(solution)/shard_map/filter_slabs/pallas_call | solution.py:131
  17.0 1.6 %collective-permute-done.4.refs_4_ = f32[256,128]{1,0:T(8,128)S(1)} collective-permute-done((f32[256,128]{1,0:T(8,128)S(1)}, f32[256,128]{1,0:T(8,128)S(1)}, u32[]{:S(2)}, u32[]{:S(2)}) %collective-permute-start.4) | collective-permute-done | bytes 131104 | tf_op jit(solution)/shard_map/ppermute | solution.py:320
  18.5 0.0 collective-permute-done.2.refs_2_
  18.5 0.0 collective-permute-done.3.refs_3_
  18.5 1.9 %sum_lags.2 = (f32[512,128]{1,0:T(8,128)S(1)}, f32[512,128]{1,0:T(8,128)S(1)}) custom-call(f32[16,1152,128]{2,1,0:T(8,128)S(1)} %filter_slabs.1.slab_ref, f32[512,128]{1,0:T(8,128)S(1)} %get-tuple-element.18.refs_0_, f32[1280,128]{1,0:T(8,128)S(1)} %collective-permute-done.near_ref.refs_2_.refs_1_, f32[512,128]{1,0:T(8,128)S(1)} %collective-permute-done.2.refs_2_, ...), custom_call_target="tpu_custom_call" | custom-call | tf_op jit(solution)/shard_map/sum_lags/pallas_call | solution.py:247
  20.4 1.6 %collective-permute-start.5 = (f32[512,128]{1,0:T(8,128)S(1)}, f32[512,128]{1,0:T(8,128)S(1)}, u32[]{:S(2)}, u32[]{:S(2)}) collective-permute-start(f32[512,128]{1,0:T(8,128)S(1)} %get-tuple-element.24), channel_id=1, source_target_pairs={{0,1},{1,0},{2,3},{3,2},{4,5},{5,4},{6,7},{7,6},{8,9},{9,8},{10,11... | collective-permute-start | bytes 786440 | tf_op jit(solution)/shard_map/ppermute | solution.py:384
  22.0 0.0 collective-permute-done.7.refs_4_
  22.0 2.2 %sum_lags.3 = (f32[256,128]{1,0:T(8,128)S(1)}, f32[256,128]{1,0:T(8,128)S(1)}, f32[256,128]{1,0:T(8,128)S(1)}, f32[256,128]{1,0:T(8,128)S(1)}) custom-call(f32[16,1152,128]{2,1,0:T(8,128)S(1)} %filter_slabs.1.slab_ref, f32[512,128]{1,0:T(8,128)S(1)} %get-tuple-element.19.refs_1_.refs_0_, f32[1280,128]{1,0:T(8,128)S(1)} %collective-permute-done.near_ref.refs_2_.refs_1_, ...), custom_call_target="tpu_custom_call" | custom-call | flops 1000000000 | bytes 10000000 | tf_op jit(solution)/shard_map/sum_lags/pallas_call | solution.py:247
  24.3 0.4 collective-permute-start.8
  24.7 1.6 %collective-permute-start.9 = (f32[256,128]{1,0:T(8,128)S(1)}, f32[256,128]{1,0:T(8,128)S(1)}, u32[]{:S(2)}, u32[]{:S(2)}) collective-permute-start(f32[256,128]{1,0:T(8,128)S(1)} %get-tuple-element.28), channel_id=1, source_target_pairs={{0,3},{1,2},{2,1},{3,0},{4,7},{5,6},{6,5},{7,4},{8,11},{9,10},{10,... | collective-permute-start | bytes 393224 | tf_op jit(solution)/shard_map/ppermute | solution.py:384
  26.2 2.5 %collective-permute-start.10 = (f32[256,128]{1,0:T(8,128)S(1)}, f32[256,128]{1,0:T(8,128)S(1)}, u32[]{:S(2)}, u32[]{:S(2)}) collective-permute-start(f32[256,128]{1,0:T(8,128)S(1)} %get-tuple-element.29), channel_id=1, source_target_pairs={{0,1},{1,0},{2,3},{3,2},{4,5},{5,4},{6,7},{7,6},{8,9},{9,8},{10,11... | collective-permute-start | bytes 393224 | tf_op jit(solution)/shard_map/ppermute | solution.py:384
  28.7 1.0 %collective-permute-done.5.came_ref.refs_1_ = f32[512,128]{1,0:T(8,128)S(1)} collective-permute-done((f32[512,128]{1,0:T(8,128)S(1)}, f32[512,128]{1,0:T(8,128)S(1)}, u32[]{:S(2)}, u32[]{:S(2)}) %collective-permute-start.5) | collective-permute-done | bytes 262176 | tf_op jit(solution)/shard_map/ppermute | solution.py:384
  29.7 0.1 collective-permute-start.6
  29.8 3.1 %collective-permute-done.8.refs_1_ = f32[256,128]{1,0:T(8,128)S(1)} collective-permute-done((f32[256,128]{1,0:T(8,128)S(1)}, f32[256,128]{1,0:T(8,128)S(1)}, u32[]{:S(2)}, u32[]{:S(2)}) %collective-permute-start.8) | collective-permute-done | bytes 131104 | tf_op jit(solution)/shard_map/ppermute | solution.py:384
  32.9 8.5 %collective-permute-done.9.refs_2_ = f32[256,128]{1,0:T(8,128)S(1)} collective-permute-done((f32[256,128]{1,0:T(8,128)S(1)}, f32[256,128]{1,0:T(8,128)S(1)}, u32[]{:S(2)}, u32[]{:S(2)}) %collective-permute-start.9) | collective-permute-done | bytes 131104 | tf_op jit(solution)/shard_map/ppermute | solution.py:384
  41.4 0.0 collective-permute-done.10.refs_3_
  41.4 0.8 %turn_back.3 = f32[2,64,256]{2,1,0:T(8,128)} custom-call(f32[256,128]{1,0:T(8,128)S(1)} %get-tuple-element.26.refs_0_, f32[256,128]{1,0:T(8,128)S(1)} %collective-permute-done.8.refs_1_, f32[256,128]{1,0:T(8,128)S(1)} %collective-permute-done.9.refs_2_, f32[256,128]{1,0:T(8,128)S(1)} %collective-permute-done.10.refs_3_), custom_call_target="tpu_custom_call" | custom-call | flops 49999998976 | bytes 10000000 | tf_op jit(solution)/shard_map/turn_back/pallas_call | solution.py:434
  42.2 1.1 %collective-permute-done.6.refs_2_ = f32[256,128]{1,0:T(8,128)S(1)} collective-permute-done((f32[256,128]{1,0:T(8,128)S(1)}, f32[256,128]{1,0:T(8,128)S(1)}, u32[]{:S(2)}, u32[]{:S(2)}) %collective-permute-start.6) | collective-permute-done | bytes 131104 | tf_op jit(solution)/shard_map/ppermute | solution.py:384
  43.3 0.8 %turn_back.2 = f32[2,64,256]{2,1,0:T(8,128)} custom-call(f32[512,128]{1,0:T(8,128)S(1)} %get-tuple-element.23.keep_ref.refs_0_.refs_5_, f32[512,128]{1,0:T(8,128)S(1)} %collective-permute-done.5.came_ref.refs_1_, f32[256,128]{1,0:T(8,128)S(1)} %collective-permute-done.6.refs_2_), custom_call_target="tpu_custom_call" | custom-call | flops 49999998976 | bytes 10000000 | tf_op jit(solution)/shard_map/turn_back/pallas_call | solution.py:434
  (1 shorter events, 0.0 us)
Async XLA Ops:
  2.7 2.2 %collective-permute-start = (f32[1280,128]{1,0:T(8,128)S(1)}, f32[1280,128]{1,0:T(8,128)S(1)}, u32[]{:S(2)}, u32[]{:S(2)}) collective-permute-start(f32[1280,128]{1,0:T(8,128)S(1)} %get-tuple-element.16), channel_id=1, source_target_pairs={{0,4},{4,0},{8,12},{12,8},{16,20},{20,16},{24,28},{28,24},{1,5},{5... | collective-permute-start | bytes 1966088 | tf_op jit(solution)/shard_map/ppermute | solution.py:320
  2.8 7.2 %collective-permute-start.1 = (f32[256,128]{1,0:T(8,128)S(1)}, f32[256,128]{1,0:T(8,128)S(1)}, u32[]{:S(2)}, u32[]{:S(2)}) collective-permute-start(f32[256,128]{1,0:T(8,128)S(1)} %get-tuple-element.17), channel_id=1, source_target_pairs={{4,8},{8,4},{12,16},{16,12},{20,24},{24,20},{28,0},{0,28},{5,9},{9... | collective-permute-start | bytes 393224 | tf_op jit(solution)/shard_map/ppermute | solution.py:347
  4.9 13.6 %collective-permute-start.2 = (f32[512,128]{1,0:T(8,128)S(1)}, f32[512,128]{1,0:T(8,128)S(1)}, u32[]{:S(2)}, u32[]{:S(2)}) collective-permute-start(f32[512,128]{1,0:T(8,128)S(1)} %get-tuple-element.20), channel_id=1, source_target_pairs={{0,8},{4,12},{8,0},{12,4},{16,24},{20,28},{24,16},{28,20},{1,9},{5... | collective-permute-start | bytes 786440 | tf_op jit(solution)/shard_map/ppermute | solution.py:320
  6.0 12.5 %collective-permute-start.3 = (f32[512,128]{1,0:T(8,128)S(1)}, f32[512,128]{1,0:T(8,128)S(1)}, u32[]{:S(2)}, u32[]{:S(2)}) collective-permute-start(f32[512,128]{1,0:T(8,128)S(1)} %get-tuple-element.21), channel_id=1, source_target_pairs={{0,16},{4,20},{8,24},{12,28},{16,0},{20,4},{24,8},{28,12},{1,17},{... | collective-permute-start | bytes 786440 | tf_op jit(solution)/shard_map/ppermute | solution.py:320
  7.1 11.5 %collective-permute-start.4 = (f32[256,128]{1,0:T(8,128)S(1)}, f32[256,128]{1,0:T(8,128)S(1)}, u32[]{:S(2)}, u32[]{:S(2)}) collective-permute-start(f32[256,128]{1,0:T(8,128)S(1)} %get-tuple-element.22), channel_id=1, source_target_pairs={{0,24},{4,28},{8,16},{12,20},{16,8},{20,12},{24,0},{28,4},{1,25},{... | collective-permute-start | bytes 393224 | tf_op jit(solution)/shard_map/ppermute | solution.py:320
  8.5 13.5 %collective-permute-start.7 = (f32[256,128]{1,0:T(8,128)S(1)}, f32[256,128]{1,0:T(8,128)S(1)}, u32[]{:S(2)}, u32[]{:S(2)}) collective-permute-start(f32[256,128]{1,0:T(8,128)S(1)} %get-tuple-element.25), channel_id=1, source_target_pairs={{0,24},{4,28},{8,16},{12,20},{16,8},{20,12},{24,0},{28,4},{1,25},{... | collective-permute-start | bytes 393224 | tf_op jit(solution)/shard_map/ppermute | solution.py:320
  20.4 9.3 %collective-permute-start.5 = (f32[512,128]{1,0:T(8,128)S(1)}, f32[512,128]{1,0:T(8,128)S(1)}, u32[]{:S(2)}, u32[]{:S(2)}) collective-permute-start(f32[512,128]{1,0:T(8,128)S(1)} %get-tuple-element.24), channel_id=1, source_target_pairs={{0,1},{1,0},{2,3},{3,2},{4,5},{5,4},{6,7},{7,6},{8,9},{9,8},{10,11... | collective-permute-start | bytes 786440 | tf_op jit(solution)/shard_map/ppermute | solution.py:384
  24.3 8.6 %collective-permute-start.8 = (f32[256,128]{1,0:T(8,128)S(1)}, f32[256,128]{1,0:T(8,128)S(1)}, u32[]{:S(2)}, u32[]{:S(2)}) collective-permute-start(f32[256,128]{1,0:T(8,128)S(1)} %get-tuple-element.27), channel_id=1, source_target_pairs={{0,2},{1,3},{2,0},{3,1},{4,6},{5,7},{6,4},{7,5},{8,10},{9,11},{10,... | collective-permute-start | bytes 393224 | tf_op jit(solution)/shard_map/ppermute | solution.py:384
  24.7 16.7 %collective-permute-start.9 = (f32[256,128]{1,0:T(8,128)S(1)}, f32[256,128]{1,0:T(8,128)S(1)}, u32[]{:S(2)}, u32[]{:S(2)}) collective-permute-start(f32[256,128]{1,0:T(8,128)S(1)} %get-tuple-element.28), channel_id=1, source_target_pairs={{0,3},{1,2},{2,1},{3,0},{4,7},{5,6},{6,5},{7,4},{8,11},{9,10},{10,... | collective-permute-start | bytes 393224 | tf_op jit(solution)/shard_map/ppermute | solution.py:384
  26.2 15.2 %collective-permute-start.10 = (f32[256,128]{1,0:T(8,128)S(1)}, f32[256,128]{1,0:T(8,128)S(1)}, u32[]{:S(2)}, u32[]{:S(2)}) collective-permute-start(f32[256,128]{1,0:T(8,128)S(1)} %get-tuple-element.29), channel_id=1, source_target_pairs={{0,1},{1,0},{2,3},{3,2},{4,5},{5,4},{6,7},{7,6},{8,9},{9,8},{10,11... | collective-permute-start | bytes 393224 | tf_op jit(solution)/shard_map/ppermute | solution.py:384
  29.7 13.6 %collective-permute-start.6 = (f32[256,128]{1,0:T(8,128)S(1)}, f32[256,128]{1,0:T(8,128)S(1)}, u32[]{:S(2)}, u32[]{:S(2)}) collective-permute-start(f32[256,128]{1,0:T(8,128)S(1)} %add_mirror.1), channel_id=1, source_target_pairs={{0,3},{1,2},{2,1},{3,0},{4,7},{5,6},{6,5},{7,4},{8,11},{9,10},{10,... | collective-permute-start | bytes 393224 | tf_op jit(solution)/shard_map/ppermute | solution.py:384

commit v3 on v2

--- a/solution.py
+++ b/solution.py
@@ -161,7 +161,7 @@
     place = lax.axis_index("lag")
     first = place * lag_count - pad
     spread = width + half
-    block_rows = ROWS * max(m for m in range(1, 11) if spread // ROWS % m == 0)
+    block_rows = ROWS * max(m for m in range(1, 14) if spread // ROWS % m == 0)
     low_at = 0 if sign > 0 else half
     high_at = half - low_at
 

time: 44.2 us -> 44.1 us (level)
  transfers between devices with their start and end apart: 11 -> 11, of which waited for: 6 -> 6; matrix products, arithmetic and copies ran while one was open for 0% -> 0% of each run, Pallas kernels for 27% -> 26%
where the time goes in v3:
time: 44.1 us; the launch traced here: 43.9 us
  waiting for transfers between devices  16.9 us (38%)
  Pallas kernels  14.4 us (33%)
  starting transfers between devices  11.9 us (27%)
  between operations  0.69 us (2%)
    ppermute x5, waiting for transfers between devices, exchange(): return lax.ppermute(parts, 'lag', [(i, i ^ distance) for i in range(count)])  13.9 us
    pallas_call x1, Pallas kernels, filter_slabs(): pl.pallas_call(functools.partial(filter_kernel, pad), out_shape=jax.Shape...  6.96 us
    ppermute x5, starting transfers between devices, exchange(): return lax.ppermute(parts, 'lag', [(i, i ^ distance) for i in range(count)])  6.17 us
    ppermute x5, starting transfers between devices, strip_swap(): lax.ppermute(part, 'strip', [(i, i ^ distance) for i in range(count)])  5.12 us
    pallas_call x2, Pallas kernels, sum_lags(): pl.pallas_call(functools.partial(sum_kernel, sign, places, where_at, BLOC...  3.79 us
    ppermute x5, waiting for transfers between devices, strip_swap(): lax.ppermute(part, 'strip', [(i, i ^ distance) for i in range(count)])  3.03 us
    pallas_call x1, Pallas kernels, gather_rows(): pl.pallas_call(functools.partial(send_kernel, pieces), out_shape=[buffer(...  2.08 us
    pallas_call x2, Pallas kernels, sum_places(): pl.pallas_call(turn_back_kernel, out_shape=jax.ShapeDtypeStruct((snaps, l...  1.52 us
  transfers between devices with their start and end apart: 11, of which 6 were waited for; matrix products, arithmetic and copies ran while one was open for 0% of the time, Pallas kernels for 26%

profile of v3, /device:TPU:18, one launch (start us, length us, event | category | flops | bytes accessed | tf_op | source)
XLA Modules:
  0.0 43.9 jit_solution(13251359532560888639)
XLA Ops:
  0.6 2.1 %send_rows.1 = (f32[1280,128]{1,0:T(8,128)S(1)}, f32[256,128]{1,0:T(8,128)S(1)}, f32[512,128]{1,0:T(8,128)S(1)}, f32[512,128]{1,0:T(8,128)S(1)}) custom-call(f32[32,64,1024]{2,1,0:T(8,128)} %grad_hbm.3, f32[2,512,128]{2,1,0:T(8,128)} %refs_0_.1, f32[2,512,128]{2,1,0:T(8,128)} %refs_1_.1), custom_call_target="tpu_custom_call" | custom-call | tf_op jit(solution)/shard_map/send_rows/pallas_call | solution.py:335
  2.7 0.1 collective-permute-start
  2.8 0.6 %collective-permute-start.1 = (f32[256,128]{1,0:T(8,128)S(1)}, f32[256,128]{1,0:T(8,128)S(1)}, u32[]{:S(2)}, u32[]{:S(2)}) collective-permute-start(f32[256,128]{1,0:T(8,128)S(1)} %get-tuple-element.17), channel_id=1, source_target_pairs={{4,8},{8,4},{12,16},{16,12},{20,24},{24,20},{28,0},{0,28},{5,9},{9... | collective-permute-start | bytes 393224 | tf_op jit(solution)/shard_map/ppermute | solution.py:347
  3.4 1.4 %collective-permute-done.near_ref.refs_2_.refs_1_ = f32[1280,128]{1,0:T(8,128)S(1)} collective-permute-done((f32[1280,128]{1,0:T(8,128)S(1)}, f32[1280,128]{1,0:T(8,128)S(1)}, u32[]{:S(2)}, u32[]{:S(2)}) %collective-permute-start) | collective-permute-done | bytes 655392 | tf_op jit(solution)/shard_map/ppermute | solution.py:320
  4.9 0.1 pack_fields.1
  4.9 1.1 %collective-permute-start.2 = (f32[512,128]{1,0:T(8,128)S(1)}, f32[512,128]{1,0:T(8,128)S(1)}, u32[]{:S(2)}, u32[]{:S(2)}) collective-permute-start(f32[512,128]{1,0:T(8,128)S(1)} %get-tuple-element.20), channel_id=1, source_target_pairs={{0,8},{4,12},{8,0},{12,4},{16,24},{20,28},{24,16},{28,20},{1,9},{5... | collective-permute-start | bytes 786440 | tf_op jit(solution)/shard_map/ppermute | solution.py:320
  6.0 1.1 %collective-permute-start.3 = (f32[512,128]{1,0:T(8,128)S(1)}, f32[512,128]{1,0:T(8,128)S(1)}, u32[]{:S(2)}, u32[]{:S(2)}) collective-permute-start(f32[512,128]{1,0:T(8,128)S(1)} %get-tuple-element.21), channel_id=1, source_target_pairs={{0,16},{4,20},{8,24},{12,28},{16,0},{20,4},{24,8},{28,12},{1,17},{... | collective-permute-start | bytes 786440 | tf_op jit(solution)/shard_map/ppermute | solution.py:320
  7.1 1.4 %collective-permute-start.4 = (f32[256,128]{1,0:T(8,128)S(1)}, f32[256,128]{1,0:T(8,128)S(1)}, u32[]{:S(2)}, u32[]{:S(2)}) collective-permute-start(f32[256,128]{1,0:T(8,128)S(1)} %get-tuple-element.22), channel_id=1, source_target_pairs={{0,24},{4,28},{8,16},{12,20},{16,8},{20,12},{24,0},{28,4},{1,25},{... | collective-permute-start | bytes 393224 | tf_op jit(solution)/shard_map/ppermute | solution.py:320
  8.5 1.5 %collective-permute-start.7 = (f32[256,128]{1,0:T(8,128)S(1)}, f32[256,128]{1,0:T(8,128)S(1)}, u32[]{:S(2)}, u32[]{:S(2)}) collective-permute-start(f32[256,128]{1,0:T(8,128)S(1)} %get-tuple-element.25), channel_id=1, source_target_pairs={{0,24},{4,28},{8,16},{12,20},{16,8},{20,12},{24,0},{28,4},{1,25},{... | collective-permute-start | bytes 393224 | tf_op jit(solution)/shard_map/ppermute | solution.py:320
  10.0 0.0 collective-permute-done.1.next_ref
  10.0 7.0 %filter_slabs.1.slab_ref = f32[16,1152,128]{2,1,0:T(8,128)S(1)} custom-call(f32[32,64,1024]{2,1,0:T(8,128)} %grad_hbm.3, f32[1280,128]{1,0:T(8,128)S(1)} %collective-permute-done.near_ref.refs_2_.refs_1_, f32[256,128]{1,0:T(8,128)S(1)} %collective-permute-done.1.next_ref), custom_call_target="tpu_custom_call" | custom-call | flops 3000000000 | bytes 10000000 | tf_op jit(solution)/shard_map/filter_slabs/pallas_call | solution.py:131
  17.0 1.6 %collective-permute-done.4.refs_4_ = f32[256,128]{1,0:T(8,128)S(1)} collective-permute-done((f32[256,128]{1,0:T(8,128)S(1)}, f32[256,128]{1,0:T(8,128)S(1)}, u32[]{:S(2)}, u32[]{:S(2)}) %collective-permute-start.4) | collective-permute-done | bytes 131104 | tf_op jit(solution)/shard_map/ppermute | solution.py:320
  18.5 0.0 collective-permute-done.2.refs_2_
  18.5 0.0 collective-permute-done.3.refs_3_
  18.5 1.7 %sum_lags.2 = (f32[512,128]{1,0:T(8,128)S(1)}, f32[512,128]{1,0:T(8,128)S(1)}) custom-call(f32[16,1152,128]{2,1,0:T(8,128)S(1)} %filter_slabs.1.slab_ref, f32[512,128]{1,0:T(8,128)S(1)} %get-tuple-element.18.refs_0_, f32[1280,128]{1,0:T(8,128)S(1)} %collective-permute-done.near_ref.refs_2_.refs_1_, f32[512,128]{1,0:T(8,128)S(1)} %collective-permute-done.2.refs_2_, ...), custom_call_target="tpu_custom_call" | custom-call | tf_op jit(solution)/shard_map/sum_lags/pallas_call | solution.py:247
  20.2 1.6 %collective-permute-start.5 = (f32[512,128]{1,0:T(8,128)S(1)}, f32[512,128]{1,0:T(8,128)S(1)}, u32[]{:S(2)}, u32[]{:S(2)}) collective-permute-start(f32[512,128]{1,0:T(8,128)S(1)} %get-tuple-element.24), channel_id=1, source_target_pairs={{0,1},{1,0},{2,3},{3,2},{4,5},{5,4},{6,7},{7,6},{8,9},{9,8},{10,11... | collective-permute-start | bytes 786440 | tf_op jit(solution)/shard_map/ppermute | solution.py:384
  21.9 0.0 collective-permute-done.7.refs_4_
  21.9 2.1 %sum_lags.3 = (f32[256,128]{1,0:T(8,128)S(1)}, f32[256,128]{1,0:T(8,128)S(1)}, f32[256,128]{1,0:T(8,128)S(1)}, f32[256,128]{1,0:T(8,128)S(1)}) custom-call(f32[16,1152,128]{2,1,0:T(8,128)S(1)} %filter_slabs.1.slab_ref, f32[512,128]{1,0:T(8,128)S(1)} %get-tuple-element.19.refs_1_.refs_0_, f32[1280,128]{1,0:T(8,128)S(1)} %collective-permute-done.near_ref.refs_2_.refs_1_, ...), custom_call_target="tpu_custom_call" | custom-call | flops 1000000000 | bytes 10000000 | tf_op jit(solution)/shard_map/sum_lags/pallas_call | solution.py:247
  24.0 0.4 collective-permute-start.8
  24.4 1.7 %collective-permute-start.9 = (f32[256,128]{1,0:T(8,128)S(1)}, f32[256,128]{1,0:T(8,128)S(1)}, u32[]{:S(2)}, u32[]{:S(2)}) collective-permute-start(f32[256,128]{1,0:T(8,128)S(1)} %get-tuple-element.28), channel_id=1, source_target_pairs={{0,3},{1,2},{2,1},{3,0},{4,7},{5,6},{6,5},{7,4},{8,11},{9,10},{10,... | collective-permute-start | bytes 393224 | tf_op jit(solution)/shard_map/ppermute | solution.py:384
  26.1 2.4 %collective-permute-start.10 = (f32[256,128]{1,0:T(8,128)S(1)}, f32[256,128]{1,0:T(8,128)S(1)}, u32[]{:S(2)}, u32[]{:S(2)}) collective-permute-start(f32[256,128]{1,0:T(8,128)S(1)} %get-tuple-element.29), channel_id=1, source_target_pairs={{0,1},{1,0},{2,3},{3,2},{4,5},{5,4},{6,7},{7,6},{8,9},{9,8},{10,11... | collective-permute-start | bytes 393224 | tf_op jit(solution)/shard_map/ppermute | solution.py:384
  28.4 1.1 %collective-permute-done.5.came_ref.refs_1_ = f32[512,128]{1,0:T(8,128)S(1)} collective-permute-done((f32[512,128]{1,0:T(8,128)S(1)}, f32[512,128]{1,0:T(8,128)S(1)}, u32[]{:S(2)}, u32[]{:S(2)}) %collective-permute-start.5) | collective-permute-done | bytes 262176 | tf_op jit(solution)/shard_map/ppermute | solution.py:384
  29.5 0.1 collective-permute-start.6
  29.6 2.7 %collective-permute-done.8.refs_1_ = f32[256,128]{1,0:T(8,128)S(1)} collective-permute-done((f32[256,128]{1,0:T(8,128)S(1)}, f32[256,128]{1,0:T(8,128)S(1)}, u32[]{:S(2)}, u32[]{:S(2)}) %collective-permute-start.8) | collective-permute-done | bytes 131104 | tf_op jit(solution)/shard_map/ppermute | solution.py:384
  32.3 8.9 %collective-permute-done.9.refs_2_ = f32[256,128]{1,0:T(8,128)S(1)} collective-permute-done((f32[256,128]{1,0:T(8,128)S(1)}, f32[256,128]{1,0:T(8,128)S(1)}, u32[]{:S(2)}, u32[]{:S(2)}) %collective-permute-start.9) | collective-permute-done | bytes 131104 | tf_op jit(solution)/shard_map/ppermute | solution.py:384
  41.2 0.0 collective-permute-done.10.refs_3_
  41.2 0.8 %turn_back.3 = f32[2,64,256]{2,1,0:T(8,128)} custom-call(f32[256,128]{1,0:T(8,128)S(1)} %get-tuple-element.26.refs_0_, f32[256,128]{1,0:T(8,128)S(1)} %collective-permute-done.8.refs_1_, f32[256,128]{1,0:T(8,128)S(1)} %collective-permute-done.9.refs_2_, f32[256,128]{1,0:T(8,128)S(1)} %collective-permute-done.10.refs_3_), custom_call_target="tpu_custom_call" | custom-call | flops 49999998976 | bytes 10000000 | tf_op jit(solution)/shard_map/turn_back/pallas_call | solution.py:434
  41.9 1.2 %collective-permute-done.6.refs_2_ = f32[256,128]{1,0:T(8,128)S(1)} collective-permute-done((f32[256,128]{1,0:T(8,128)S(1)}, f32[256,128]{1,0:T(8,128)S(1)}, u32[]{:S(2)}, u32[]{:S(2)}) %collective-permute-start.6) | collective-permute-done | bytes 131104 | tf_op jit(solution)/shard_map/ppermute | solution.py:384
  43.2 0.8 %turn_back.2 = f32[2,64,256]{2,1,0:T(8,128)} custom-call(f32[512,128]{1,0:T(8,128)S(1)} %get-tuple-element.23.keep_ref.refs_0_.refs_5_, f32[512,128]{1,0:T(8,128)S(1)} %collective-permute-done.5.came_ref.refs_1_, f32[256,128]{1,0:T(8,128)S(1)} %collective-permute-done.6.refs_2_), custom_call_target="tpu_custom_call" | custom-call | flops 49999998976 | bytes 10000000 | tf_op jit(solution)/shard_map/turn_back/pallas_call | solution.py:434
  (1 shorter events, 0.0 us)
Async XLA Ops:
  2.7 2.2 %collective-permute-start = (f32[1280,128]{1,0:T(8,128)S(1)}, f32[1280,128]{1,0:T(8,128)S(1)}, u32[]{:S(2)}, u32[]{:S(2)}) collective-permute-start(f32[1280,128]{1,0:T(8,128)S(1)} %get-tuple-element.16), channel_id=1, source_target_pairs={{0,4},{4,0},{8,12},{12,8},{16,20},{20,16},{24,28},{28,24},{1,5},{5... | collective-permute-start | bytes 1966088 | tf_op jit(solution)/shard_map/ppermute | solution.py:320
  2.8 7.2 %collective-permute-start.1 = (f32[256,128]{1,0:T(8,128)S(1)}, f32[256,128]{1,0:T(8,128)S(1)}, u32[]{:S(2)}, u32[]{:S(2)}) collective-permute-start(f32[256,128]{1,0:T(8,128)S(1)} %get-tuple-element.17), channel_id=1, source_target_pairs={{4,8},{8,4},{12,16},{16,12},{20,24},{24,20},{28,0},{0,28},{5,9},{9... | collective-permute-start | bytes 393224 | tf_op jit(solution)/shard_map/ppermute | solution.py:347
  4.9 13.6 %collective-permute-start.2 = (f32[512,128]{1,0:T(8,128)S(1)}, f32[512,128]{1,0:T(8,128)S(1)}, u32[]{:S(2)}, u32[]{:S(2)}) collective-permute-start(f32[512,128]{1,0:T(8,128)S(1)} %get-tuple-element.20), channel_id=1, source_target_pairs={{0,8},{4,12},{8,0},{12,4},{16,24},{20,28},{24,16},{28,20},{1,9},{5... | collective-permute-start | bytes 786440 | tf_op jit(solution)/shard_map/ppermute | solution.py:320
  6.0 12.5 %collective-permute-start.3 = (f32[512,128]{1,0:T(8,128)S(1)}, f32[512,128]{1,0:T(8,128)S(1)}, u32[]{:S(2)}, u32[]{:S(2)}) collective-permute-start(f32[512,128]{1,0:T(8,128)S(1)} %get-tuple-element.21), channel_id=1, source_target_pairs={{0,16},{4,20},{8,24},{12,28},{16,0},{20,4},{24,8},{28,12},{1,17},{... | collective-permute-start | bytes 786440 | tf_op jit(solution)/shard_map/ppermute | solution.py:320
  7.1 11.5 %collective-permute-start.4 = (f32[256,128]{1,0:T(8,128)S(1)}, f32[256,128]{1,0:T(8,128)S(1)}, u32[]{:S(2)}, u32[]{:S(2)}) collective-permute-start(f32[256,128]{1,0:T(8,128)S(1)} %get-tuple-element.22), channel_id=1, source_target_pairs={{0,24},{4,28},{8,16},{12,20},{16,8},{20,12},{24,0},{28,4},{1,25},{... | collective-permute-start | bytes 393224 | tf_op jit(solution)/shard_map/ppermute | solution.py:320
  8.5 13.4 %collective-permute-start.7 = (f32[256,128]{1,0:T(8,128)S(1)}, f32[256,128]{1,0:T(8,128)S(1)}, u32[]{:S(2)}, u32[]{:S(2)}) collective-permute-start(f32[256,128]{1,0:T(8,128)S(1)} %get-tuple-element.25), channel_id=1, source_target_pairs={{0,24},{4,28},{8,16},{12,20},{16,8},{20,12},{24,0},{28,4},{1,25},{... | collective-permute-start | bytes 393224 | tf_op jit(solution)/shard_map/ppermute | solution.py:320
  20.2 9.3 %collective-permute-start.5 = (f32[512,128]{1,0:T(8,128)S(1)}, f32[512,128]{1,0:T(8,128)S(1)}, u32[]{:S(2)}, u32[]{:S(2)}) collective-permute-start(f32[512,128]{1,0:T(8,128)S(1)} %get-tuple-element.24), channel_id=1, source_target_pairs={{0,1},{1,0},{2,3},{3,2},{4,5},{5,4},{6,7},{7,6},{8,9},{9,8},{10,11... | collective-permute-start | bytes 786440 | tf_op jit(solution)/shard_map/ppermute | solution.py:384
  24.0 8.3 %collective-permute-start.8 = (f32[256,128]{1,0:T(8,128)S(1)}, f32[256,128]{1,0:T(8,128)S(1)}, u32[]{:S(2)}, u32[]{:S(2)}) collective-permute-start(f32[256,128]{1,0:T(8,128)S(1)} %get-tuple-element.27), channel_id=1, source_target_pairs={{0,2},{1,3},{2,0},{3,1},{4,6},{5,7},{6,4},{7,5},{8,10},{9,11},{10,... | collective-permute-start | bytes 393224 | tf_op jit(solution)/shard_map/ppermute | solution.py:384
  24.4 16.8 %collective-permute-start.9 = (f32[256,128]{1,0:T(8,128)S(1)}, f32[256,128]{1,0:T(8,128)S(1)}, u32[]{:S(2)}, u32[]{:S(2)}) collective-permute-start(f32[256,128]{1,0:T(8,128)S(1)} %get-tuple-element.28), channel_id=1, source_target_pairs={{0,3},{1,2},{2,1},{3,0},{4,7},{5,6},{6,5},{7,4},{8,11},{9,10},{10,... | collective-permute-start | bytes 393224 | tf_op jit(solution)/shard_map/ppermute | solution.py:384
  26.1 15.1 %collective-permute-start.10 = (f32[256,128]{1,0:T(8,128)S(1)}, f32[256,128]{1,0:T(8,128)S(1)}, u32[]{:S(2)}, u32[]{:S(2)}) collective-permute-start(f32[256,128]{1,0:T(8,128)S(1)} %get-tuple-element.29), channel_id=1, source_target_pairs={{0,1},{1,0},{2,3},{3,2},{4,5},{5,4},{6,7},{7,6},{8,9},{9,8},{10,11... | collective-permute-start | bytes 393224 | tf_op jit(solution)/shard_map/ppermute | solution.py:384
  29.5 13.6 %collective-permute-start.6 = (f32[256,128]{1,0:T(8,128)S(1)}, f32[256,128]{1,0:T(8,128)S(1)}, u32[]{:S(2)}, u32[]{:S(2)}) collective-permute-start(f32[256,128]{1,0:T(8,128)S(1)} %add_mirror.1), channel_id=1, source_target_pairs={{0,3},{1,2},{2,1},{3,0},{4,7},{5,6},{6,5},{7,4},{8,11},{9,10},{10,... | collective-permute-start | bytes 393224 | tf_op jit(solution)/shard_map/ppermute | solution.py:384
